TPU v7x, 32 devices: a whole 2x2x4 slice. The times are simulated.
32 devices in a mesh: grp: 4 (over y, core), wide: 4 (over z), tp: 2 (over x).
Axes of the slice: x: 2, y: 2, z: 4, core: 2. Of those that a mesh axis runs over, the one named last changes fastest.
Arguments:
- layer_input: bfloat16 [4096, 768], P(('grp', 'wide')), may hold values from -6 to 6
- memory: bfloat16 [4096, 768], P(('grp', 'wide')), may hold values from -6 to 6
- reader_map: int32 [4096], P('grp'), may hold values from 0 to 3, as said below
- target_ids: int32 [4096], P('grp'), may hold values from 0 to 32127
- target_lengths: int32 [16], replicated, may hold values from 128 to 256, as said below
- out_grad: bfloat16 [4096, 768], P(('grp', 'wide')), may hold values from -0.00036621094 to 0.00036621094
- self_q: bfloat16 [768, 768], P('wide', 'tp'), may hold values from -0.21875 to 0.21875
- self_k: bfloat16 [768, 768], P('wide', 'tp'), may hold values from -0.21875 to 0.21875
- self_v: bfloat16 [768, 768], P('wide', 'tp'), may hold values from -0.21875 to 0.21875
- self_o: bfloat16 [768, 768], P('wide', 'tp'), may hold values from -0.75 to 0.75
- cross_q: bfloat16 [768, 768], P('wide', 'tp'), may hold values from -0.21875 to 0.21875
- cross_k: bfloat16 [768, 768], P('wide', 'tp'), may hold values from -0.21875 to 0.21875
- cross_v: bfloat16 [768, 768], P('wide', 'tp'), may hold values from -0.21875 to 0.21875
- cross_o: bfloat16 [768, 768], P('wide', 'tp'), may hold values from -0.75 to 0.75
- ff_gate: bfloat16 [768, 2048], P('wide', 'tp'), may hold values from -0.21875 to 0.21875
- ff_up: bfloat16 [768, 2048], P('wide', 'tp'), may hold values from -0.21875 to 0.21875
- ff_out: bfloat16 [768, 2048], P('wide', 'tp'), may hold values from -0.125 to 0.125
- gain_self: bfloat16 [768], P('wide'), may hold values from 0.099609375 to 1.8984375
- gain_cross: bfloat16 [768], P('wide'), may hold values from 0.099609375 to 1.8984375
- gain_ff: bfloat16 [768], P('wide'), may hold values from 0.099609375 to 1.8984375
- gain_exit: bfloat16 [768], P('wide'), may hold values from 0.099609375 to 1.8984375
- exit_table: bfloat16 [32128, 768], P(('wide', 'tp')), may hold values from -9 to 9
Outputs:
- block_output: bfloat16 [4096, 768], P(('grp', 'wide'))
- loss: float32 [], replicated
- input_grad: float32 [4096, 768], P(('grp', 'wide'))
- memory_grad: float32 [4096, 768], P(('grp', 'wide'))
- self_q_grad: float32 [768, 768], P('wide', 'tp')
- self_k_grad: float32 [768, 768], P('wide', 'tp')
- self_v_grad: float32 [768, 768], P('wide', 'tp')
- self_o_grad: float32 [768, 768], P('wide', 'tp')
- cross_q_grad: float32 [768, 768], P('wide', 'tp')
- cross_k_grad: float32 [768, 768], P('wide', 'tp')
- cross_v_grad: float32 [768, 768], P('wide', 'tp')
- cross_o_grad: float32 [768, 768], P('wide', 'tp')
- ff_gate_grad: float32 [768, 2048], P('wide', 'tp')
- ff_up_grad: float32 [768, 2048], P('wide', 'tp')
- ff_out_grad: float32 [768, 2048], P('wide', 'tp')
- gain_self_grad: float32 [768], P('wide')
- gain_cross_grad: float32 [768], P('wide')
- gain_ff_grad: float32 [768], P('wide')
- gain_exit_grad: float32 [768], P('wide')
- exit_grad: float32 [32128, 768], P(('wide', 'tp'))
Inputs may be any that keep to these rules, and one draw needn't show every extreme that they name: `reader_map`: each memory row is read by exactly one target sequence of its group; every sequence reads at least one row of its group; of the 256 rows held by one device, at most 128 are read by one sequence, and in each group one sequence reads exactly 128 rows held on every device of wide. `target_lengths`: some sequence has the full length 256.
All inputs are finite; a program needn't handle non-finite values.
Results may differ from a plain program's by a relative error of at most 0.03.
Values may be sent and summed in bfloat16 or wider, within the bound.
A program may use at most 192 MiB of HBM per device.

v0:
```python
import functools
import types

import jax
import jax.numpy as jnp
from jax import lax
from jax.experimental import pallas as pl
from jax.experimental.pallas import tpu as pltpu
from jax.sharding import PartitionSpec as P

HEAD_DIM = 64


EPSILON = 1e-06
MASKED = -1e30


def merged(shard, axis, combine):
    everything = jax.tree.map(
        lambda part, kind: lax.all_gather(part.astype(kind), axis),
        shard,
        (jnp.bfloat16, jnp.bfloat16, jnp.bfloat16),
    )

    def take(k):
        return jax.tree.map(lambda part, own: part[k].astype(own.dtype), everything, shard)

    return lax.fori_loop(
        1, lax.axis_size(axis), lambda k, so_far: combine(so_far, take(k)), take(0)
    )


def project(left, right):
    return jnp.dot(left, right, preferred_element_type=jnp.float32)


def project_back(left, right):
    return lax.dot_general(
        left, right, (((1,), (1,)), ((), ())), preferred_element_type=jnp.float32
    )


def outer_rows(left, right):
    return lax.dot_general(
        left, right, (((0,), (0,)), ((), ())), preferred_element_type=jnp.float32
    )


def smooth_gate(values):
    return jax.nn.gelu(values, approximate=True)


def normalize(values, gain):
    factor = lax.rsqrt(jnp.mean(values * values, axis=1, keepdims=True) + EPSILON)
    unit_rows = values * factor
    return ((unit_rows * gain).astype(jnp.bfloat16), unit_rows, factor)


def normalize_back(values, unit_rows, factor, gain, grad_rows):
    gain_grad = jnp.sum(grad_rows * unit_rows, axis=0)
    scaled = grad_rows * gain
    inner = jnp.mean(scaled * values, axis=1, keepdims=True)
    return (gain_grad, factor * scaled - unit_rows * factor * factor * inner)


def split_heads(values):
    return values.reshape(values.shape[0], -1, HEAD_DIM).transpose(1, 0, 2)


def join_heads(values):
    return values.transpose(1, 0, 2).reshape(values.shape[1], -1)


def read_slots(group_map, reader, holders, rows_each, capacity):
    matched = (group_map.reshape(holders, rows_each) == reader).astype(jnp.int32)
    ranks = jnp.cumsum(matched, axis=1) - 1
    counts = jnp.sum(matched, axis=1)
    place = lax.iota(jnp.int32, holders * capacity)
    valid = place % capacity < jnp.repeat(counts, capacity, total_repeat_length=holders * capacity)
    anchor = lax.iota(jnp.int32, holders)[:, None] * capacity + ranks
    target = jnp.where(matched > 0, anchor, holders * capacity)
    return (valid, target.reshape(-1))


def attend_forward(queries, keys, values, allowed):
    factor = HEAD_DIM ** (-0.5)

    def one_head(parts):
        query, key_rows, value_rows = parts
        scores = jnp.where(allowed, project_back(query, key_rows) * factor, MASKED)
        highest = jnp.max(scores, axis=1, keepdims=True)
        exponent = jnp.exp(scores - highest)
        total = jnp.sum(exponent, axis=1, keepdims=True)
        soft_weights = (exponent / total).astype(jnp.bfloat16)
        return (project(soft_weights, value_rows), (highest + jnp.log(total))[:, 0])

    context, log_total = lax.map(
        one_head, (split_heads(queries), split_heads(keys), split_heads(values))
    )
    return (join_heads(context).astype(jnp.bfloat16), log_total)


def attend_backward(queries, keys, values, context_grad, log_total, allowed):
    factor = HEAD_DIM ** (-0.5)

    def one_head(parts):
        query, key_rows, value_rows, grad_rows, log_row = parts
        scores = jnp.where(allowed, project_back(query, key_rows) * factor, MASKED)
        soft = jnp.exp(scores - log_row[:, None])
        soft_grad = project_back(grad_rows, value_rows)
        score_grad = (soft * (soft_grad - jnp.sum(soft * soft_grad, axis=1, keepdims=True))).astype(
            jnp.bfloat16
        )
        query_grad = project(score_grad, key_rows) * factor
        key_grad = outer_rows(score_grad, query) * factor
        value_grad = outer_rows(soft.astype(jnp.bfloat16), grad_rows)
        return (query_grad, key_grad, value_grad)

    grads = lax.map(
        one_head,
        (
            split_heads(queries),
            split_heads(keys),
            split_heads(values),
            split_heads(context_grad),
            log_total,
        ),
    )
    return (join_heads(grads[0]), join_heads(grads[1]), join_heads(grads[2]))


def heads_total(partial_rows):
    return lax.psum(partial_rows, "tp")


def input_total(partial_rows):
    return lax.psum(partial_rows.astype(jnp.bfloat16), "tp").astype(jnp.float32)


def merge_softmax(first, second):
    highest = jnp.maximum(first[0], second[0])
    total = first[1] * jnp.exp(first[0] - highest) + second[1] * jnp.exp(second[0] - highest)
    return (highest, total, first[2] + second[2])


def plain_body(
    layer_input,
    memory,
    reader_map,
    target_ids,
    target_lengths,
    out_grad,
    self_q,
    self_k,
    self_v,
    self_o,
    cross_q,
    cross_k,
    cross_v,
    cross_o,
    ff_gate,
    ff_up,
    ff_out,
    gain_self,
    gain_cross,
    gain_ff,
    gain_exit,
    exit_table,
):
    (
        w_query,
        w_key,
        w_value,
        w_output,
        c_query,
        c_key,
        c_value,
        c_output,
        w_gate,
        w_up,
        w_down,
        full_gain_self,
        full_gain_cross,
        full_gain_ff,
        full_gain_exit,
    ) = (
        lax.all_gather(self_q, "wide", axis=0, tiled=True),
        lax.all_gather(self_k, "wide", axis=0, tiled=True),
        lax.all_gather(self_v, "wide", axis=0, tiled=True),
        lax.all_gather(self_o, "wide", axis=0, tiled=True),
        lax.all_gather(cross_q, "wide", axis=0, tiled=True),
        lax.all_gather(cross_k, "wide", axis=0, tiled=True),
        lax.all_gather(cross_v, "wide", axis=0, tiled=True),
        lax.all_gather(cross_o, "wide", axis=0, tiled=True),
        lax.all_gather(ff_gate, "wide", axis=0, tiled=True),
        lax.all_gather(ff_up, "wide", axis=0, tiled=True),
        lax.all_gather(ff_out, "wide", axis=0, tiled=True),
        lax.all_gather(gain_self, "wide", axis=0, tiled=True),
        lax.all_gather(gain_cross, "wide", axis=0, tiled=True),
        lax.all_gather(gain_ff, "wide", axis=0, tiled=True),
        lax.all_gather(gain_exit, "wide", axis=0, tiled=True),
    )
    gain_one = full_gain_self.astype(jnp.float32)
    gain_two = full_gain_cross.astype(jnp.float32)
    gain_three = full_gain_ff.astype(jnp.float32)
    gain_last = full_gain_exit.astype(jnp.float32)
    seq_rows = layer_input.shape[0]
    wide_count = lax.axis_size("wide")
    wide_index = lax.axis_index("wide")
    group_index = lax.axis_index("grp")
    group_lengths = lax.dynamic_slice_in_dim(target_lengths, group_index * wide_count, wide_count)
    own_length = lax.dynamic_index_in_dim(group_lengths, wide_index, keepdims=False)
    hidden = layer_input.astype(jnp.float32)
    norm_self, unit_self, factor_self = normalize(hidden, gain_one)
    queries = project(norm_self, w_query).astype(jnp.bfloat16)
    keys = project(norm_self, w_key).astype(jnp.bfloat16)
    values = project(norm_self, w_value).astype(jnp.bfloat16)
    position = lax.iota(jnp.int32, seq_rows)
    allowed_self = (position[None, :] <= position[:, None]) & (position[None, :] < own_length)
    context_self, log_self = attend_forward(queries, keys, values, allowed_self)
    resid_one = hidden + heads_total(project_back(context_self, w_output))
    norm_cross, unit_cross, factor_cross = normalize(resid_one, gain_two)
    cross_queries = project(norm_cross, c_query).astype(jnp.bfloat16)
    memory_keys = project(memory, c_key).astype(jnp.bfloat16)
    memory_values = project(memory, c_value).astype(jnp.bfloat16)
    rows_each = memory.shape[0]
    capacity = max(2, 2 * rows_each // wide_count)
    slot_count = wide_count * capacity
    slot_valid, slot_target = read_slots(reader_map, wide_index, wide_count, rows_each, capacity)
    keys_all, values_all = (
        lax.all_gather(memory_keys, "wide", axis=0, tiled=True),
        lax.all_gather(memory_values, "wide", axis=0, tiled=True),
    )
    read_table = (
        jnp.zeros((slot_count,), jnp.int32)
        .at[slot_target]
        .set(lax.iota(jnp.int32, wide_count * rows_each), mode="drop")
    )
    keys_read = jnp.take(keys_all, read_table, axis=0)
    values_read = jnp.take(values_all, read_table, axis=0)
    allowed_cross = slot_valid[None, :]
    context_cross, log_cross = attend_forward(cross_queries, keys_read, values_read, allowed_cross)
    resid_two = resid_one + heads_total(project_back(context_cross, c_output))
    norm_ff, unit_ff, factor_ff = normalize(resid_two, gain_three)
    gate_float = project(norm_ff, w_gate).astype(jnp.bfloat16).astype(jnp.float32)
    up_float = project(norm_ff, w_up).astype(jnp.bfloat16).astype(jnp.float32)
    gelu_value, gelu_pull = jax.vjp(smooth_gate, gate_float)
    ff_hidden = (gelu_value * up_float).astype(jnp.bfloat16)
    resid_three = resid_two + heads_total(project_back(ff_hidden, w_down))
    block_output = resid_three.astype(jnp.bfloat16)
    norm_exit, unit_exit, factor_exit = normalize(resid_three, gain_last)
    rows_all = lax.all_gather(norm_exit, "wide", axis=0, tiled=True)
    group_tokens = rows_all.shape[0]
    vocab_rows = exit_table.shape[0]
    scale_exit = float(rows_all.shape[1]) ** (-0.5)
    logits = project_back(rows_all, exit_table) * scale_exit
    vocab_ids = lax.axis_index(("wide", "tp")) * vocab_rows + lax.iota(jnp.int32, vocab_rows)
    is_target = target_ids[:, None] == vocab_ids[None, :]
    local_high = jnp.max(logits, axis=1)
    local_total = jnp.sum(jnp.exp(logits - local_high[:, None]), axis=1)
    local_pick = jnp.sum(jnp.where(is_target, logits, 0.0), axis=1)
    highest, total_exp, target_logit = merged(
        (local_high, local_total, local_pick), ("wide", "tp"), merge_softmax
    )
    log_total = highest + jnp.log(total_exp)
    token_place = lax.iota(jnp.int32, group_tokens)
    valid = token_place % seq_rows < jnp.repeat(
        group_lengths, seq_rows, total_repeat_length=group_tokens
    )
    token_count = jnp.sum(target_lengths).astype(jnp.float32)
    token_weight = jnp.where(valid, 1.0, 0.0).astype(jnp.float32) / token_count
    group_loss = jnp.sum(token_weight * (log_total - target_logit))
    logit_grad = (
        (jnp.exp(logits - log_total[:, None]) - jnp.where(is_target, 1.0, 0.0))
        * token_weight[:, None]
    ).astype(jnp.bfloat16)
    rows_grad_all = project(logit_grad, exit_table) * scale_exit
    exit_grad = outer_rows(logit_grad, rows_all) * scale_exit
    rows_part = lax.psum_scatter(
        rows_grad_all.astype(jnp.bfloat16), "wide", scatter_dimension=0, tiled=True
    )
    norm_exit_grad = lax.psum(rows_part, "tp").astype(jnp.float32)
    gain_exit_grad, back_exit = normalize_back(
        resid_three, unit_exit, factor_exit, gain_last, norm_exit_grad
    )
    resid_three_grad = out_grad.astype(jnp.float32) + back_exit
    ff_branch = resid_three_grad.astype(jnp.bfloat16)
    w_down_grad = outer_rows(ff_branch, ff_hidden)
    hidden_grad = project(ff_branch, w_down)
    gate_grad = gelu_pull(hidden_grad * up_float)[0].astype(jnp.bfloat16)
    up_grad = (hidden_grad * gelu_value).astype(jnp.bfloat16)
    w_gate_grad = outer_rows(norm_ff, gate_grad)
    w_up_grad = outer_rows(norm_ff, up_grad)
    norm_ff_grad = input_total(project_back(gate_grad, w_gate) + project_back(up_grad, w_up))
    gain_ff_grad, back_ff = normalize_back(resid_two, unit_ff, factor_ff, gain_three, norm_ff_grad)
    resid_two_grad = resid_three_grad + back_ff
    cross_branch = resid_two_grad.astype(jnp.bfloat16)
    c_output_grad = outer_rows(cross_branch, context_cross)
    cross_context_grad = project(cross_branch, c_output).astype(jnp.bfloat16)
    cross_query_grad, keys_grad_read, values_grad_read = attend_backward(
        cross_queries, keys_read, values_read, cross_context_grad, log_cross, allowed_cross
    )
    empty_grads = jnp.zeros((wide_count * rows_each, keys_grad_read.shape[1]), jnp.float32)
    keys_grad_all = empty_grads.at[read_table].add(keys_grad_read)
    values_grad_all = empty_grads.at[read_table].add(values_grad_read)
    keys_grad, values_grad = (
        lax.psum_scatter(
            keys_grad_all.astype(jnp.bfloat16), "wide", scatter_dimension=0, tiled=True
        ).astype(jnp.float32),
        lax.psum_scatter(
            values_grad_all.astype(jnp.bfloat16), "wide", scatter_dimension=0, tiled=True
        ).astype(jnp.float32),
    )
    keys_grad = keys_grad.astype(jnp.bfloat16)
    values_grad = values_grad.astype(jnp.bfloat16)
    cross_query_grad = cross_query_grad.astype(jnp.bfloat16)
    c_query_grad = outer_rows(norm_cross, cross_query_grad)
    c_key_grad = outer_rows(memory, keys_grad)
    c_value_grad = outer_rows(memory, values_grad)
    norm_cross_grad, memory_grad = (
        lax.psum(project_back(cross_query_grad, c_query).astype(jnp.bfloat16), "tp").astype(
            jnp.float32
        ),
        lax.psum(
            (project_back(keys_grad, c_key) + project_back(values_grad, c_value)).astype(
                jnp.bfloat16
            ),
            "tp",
        ).astype(jnp.float32),
    )
    gain_cross_grad, back_cross = normalize_back(
        resid_one, unit_cross, factor_cross, gain_two, norm_cross_grad
    )
    resid_one_grad = resid_two_grad + back_cross
    self_branch = resid_one_grad.astype(jnp.bfloat16)
    w_output_grad = outer_rows(self_branch, context_self)
    self_context_grad = project(self_branch, w_output).astype(jnp.bfloat16)
    query_grad, key_grad, value_grad = attend_backward(
        queries, keys, values, self_context_grad, log_self, allowed_self
    )
    query_grad = query_grad.astype(jnp.bfloat16)
    key_grad = key_grad.astype(jnp.bfloat16)
    value_grad = value_grad.astype(jnp.bfloat16)
    w_query_grad = outer_rows(norm_self, query_grad)
    w_key_grad = outer_rows(norm_self, key_grad)
    w_value_grad = outer_rows(norm_self, value_grad)
    norm_self_grad = input_total(
        project_back(query_grad, w_query)
        + project_back(key_grad, w_key)
        + project_back(value_grad, w_value)
    )
    gain_self_grad, back_self = normalize_back(
        hidden, unit_self, factor_self, gain_one, norm_self_grad
    )
    input_grad = resid_one_grad + back_self
    shards = (
        lax.psum_scatter(
            w_query_grad.astype(jnp.bfloat16), "wide", scatter_dimension=0, tiled=True
        ).astype(jnp.float32),
        lax.psum_scatter(
            w_key_grad.astype(jnp.bfloat16), "wide", scatter_dimension=0, tiled=True
        ).astype(jnp.float32),
        lax.psum_scatter(
            w_value_grad.astype(jnp.bfloat16), "wide", scatter_dimension=0, tiled=True
        ).astype(jnp.float32),
        lax.psum_scatter(
            w_output_grad.astype(jnp.bfloat16), "wide", scatter_dimension=0, tiled=True
        ).astype(jnp.float32),
        lax.psum_scatter(
            c_query_grad.astype(jnp.bfloat16), "wide", scatter_dimension=0, tiled=True
        ).astype(jnp.float32),
        lax.psum_scatter(
            c_key_grad.astype(jnp.bfloat16), "wide", scatter_dimension=0, tiled=True
        ).astype(jnp.float32),
        lax.psum_scatter(
            c_value_grad.astype(jnp.bfloat16), "wide", scatter_dimension=0, tiled=True
        ).astype(jnp.float32),
        lax.psum_scatter(
            c_output_grad.astype(jnp.bfloat16), "wide", scatter_dimension=0, tiled=True
        ).astype(jnp.float32),
        lax.psum_scatter(
            w_gate_grad.astype(jnp.bfloat16), "wide", scatter_dimension=0, tiled=True
        ).astype(jnp.float32),
        lax.psum_scatter(
            w_up_grad.astype(jnp.bfloat16), "wide", scatter_dimension=0, tiled=True
        ).astype(jnp.float32),
        lax.psum_scatter(
            w_down_grad.astype(jnp.bfloat16), "wide", scatter_dimension=0, tiled=True
        ).astype(jnp.float32),
        lax.psum_scatter(
            gain_self_grad.astype(jnp.bfloat16), "wide", scatter_dimension=0, tiled=True
        ).astype(jnp.float32),
        lax.psum_scatter(
            gain_cross_grad.astype(jnp.bfloat16), "wide", scatter_dimension=0, tiled=True
        ).astype(jnp.float32),
        lax.psum_scatter(
            gain_ff_grad.astype(jnp.bfloat16), "wide", scatter_dimension=0, tiled=True
        ).astype(jnp.float32),
        lax.psum_scatter(
            gain_exit_grad.astype(jnp.bfloat16), "wide", scatter_dimension=0, tiled=True
        ).astype(jnp.float32),
    )
    totals = (
        lax.psum(shards[0].astype(jnp.bfloat16), "grp").astype(jnp.float32),
        lax.psum(shards[1].astype(jnp.bfloat16), "grp").astype(jnp.float32),
        lax.psum(shards[2].astype(jnp.bfloat16), "grp").astype(jnp.float32),
        lax.psum(shards[3].astype(jnp.bfloat16), "grp").astype(jnp.float32),
        lax.psum(shards[4].astype(jnp.bfloat16), "grp").astype(jnp.float32),
        lax.psum(shards[5].astype(jnp.bfloat16), "grp").astype(jnp.float32),
        lax.psum(shards[6].astype(jnp.bfloat16), "grp").astype(jnp.float32),
        lax.psum(shards[7].astype(jnp.bfloat16), "grp").astype(jnp.float32),
        lax.psum(shards[8].astype(jnp.bfloat16), "grp").astype(jnp.float32),
        lax.psum(shards[9].astype(jnp.bfloat16), "grp").astype(jnp.float32),
        lax.psum(shards[10].astype(jnp.bfloat16), "grp").astype(jnp.float32),
        lax.psum(shards[11].astype(jnp.bfloat16), "grp").astype(jnp.float32),
        lax.psum(shards[12].astype(jnp.bfloat16), "grp").astype(jnp.float32),
        lax.psum(shards[13].astype(jnp.bfloat16), "grp").astype(jnp.float32),
        lax.psum(shards[14].astype(jnp.bfloat16), "grp").astype(jnp.float32),
        lax.psum(exit_grad.astype(jnp.bfloat16), "grp").astype(jnp.float32),
        lax.psum(group_loss.astype(jnp.bfloat16), "grp").astype(jnp.float32),
    )
    return (
        block_output,
        totals[16],
        input_grad,
        memory_grad,
        totals[0],
        totals[1],
        totals[2],
        totals[3],
        totals[4],
        totals[5],
        totals[6],
        totals[7],
        totals[8],
        totals[9],
        totals[10],
        totals[11],
        totals[12],
        totals[13],
        totals[14],
        totals[15],
    )


MESH = pl.DeviceIdType.MESH
BF = jnp.bfloat16
F32 = jnp.float32
VMEM_BYTES = 63 << 20


def dot_nn(left, right):
    return lax.dot_general(left, right, (((1,), (0,)), ((), ())), preferred_element_type=F32)


def dot_nt(left, right):
    return lax.dot_general(left, right, (((1,), (1,)), ((), ())), preferred_element_type=F32)


def dot_tn(left, right):
    return lax.dot_general(left, right, (((0,), (0,)), ((), ())), preferred_element_type=F32)


class Move:
    def __init__(self, out, arrival):
        self.out, self.arrival = out, arrival

    def start(self):
        self.out.start()
        return self

    def sent(self):
        self.out.wait_send()

    def landed(self):
        self.arrival.wait_recv()


class Links:
    def __init__(self, send_sems, recv_sems):
        self.send_sems, self.recv_sems = send_sems, recv_sems
        self.used = 0
        self.moves = []

    def move(self, src, dst, device, lands):
        k = self.used
        self.used += 1
        out = pltpu.make_async_remote_copy(
            src_ref=src, dst_ref=dst, send_sem=self.send_sems.at[k], recv_sem=self.recv_sems.at[k],
            device_id=device, device_id_type=MESH,
        )
        arrival = pltpu.make_async_remote_copy(
            src_ref=lands, dst_ref=lands, send_sem=self.send_sems.at[k], recv_sem=self.recv_sems.at[k],
            device_id=device, device_id_type=MESH,
        )
        made = Move(out, arrival)
        self.moves.append(made)
        return made

    def finish(self):
        for made in self.moves:
            made.sent()

    def finish_rest(self, done):
        for made in self.moves:
            if made not in done:
                made.sent()


class Copies:
    def __init__(self, sems):
        self.sems, self.used, self.pending = sems, 0, []

    def start(self, src, dst):
        made = pltpu.make_async_copy(src, dst, self.sems.at[self.used])
        self.used += 1
        made.start()
        return made

    def save(self, src, dst):
        self.pending.append(self.start(src, dst))

    def finish(self):
        for made in self.pending:
            made.wait()


def greet(devices):
    barrier = pltpu.get_barrier_semaphore()
    for device in devices:
        pl.semaphore_signal(barrier, inc=1, device_id=device, device_id_type=MESH)
    pl.semaphore_wait(barrier, len(devices))


def position(count):
    g, w, t = lax.axis_index("grp"), lax.axis_index("wide"), lax.axis_index("tp")
    c = lax.rem(g, 2)
    left, right, far = (lax.rem(w + d, count) for d in (count - 1, 1, 2))
    return types.SimpleNamespace(
        count=count, g=g, w=w, t=t, c=c, yy=lax.div(g, 2), left=left, right=right, far=far,
        to_left={"wide": left}, to_right={"wide": right}, to_far={"wide": far},
        to_core={"grp": g + 1 - 2 * c}, to_y={"grp": lax.rem(g + 2, 4)}, to_tp={"tp": 1 - t},
    )


def rms_rows(values, gain):
    factor = lax.rsqrt(jnp.mean(values * values, axis=1, keepdims=True) + EPSILON)
    return (values * factor * gain).astype(BF)


def lane_masks():
    lane = lax.broadcasted_iota(jnp.int32, (1, 2 * HEAD_DIM), 1)
    low = jnp.where(lane < HEAD_DIM, 1.0, 0.0).astype(F32)
    return low.astype(BF), (1.0 - low).astype(BF)


def both_heads(pair):
    low, high = lane_masks()
    return jnp.concatenate([pair * low, pair * high], axis=0)


def pick_heads(stacked):
    rows = stacked.shape[0] // 2
    lane = lax.broadcasted_iota(jnp.int32, (rows, 2 * HEAD_DIM), 1)
    return jnp.where(lane < HEAD_DIM, stacked[:rows], stacked[rows:])


def pair_columns(p):
    return pl.ds(pl.multiple_of(p * 2 * HEAD_DIM, 2 * HEAD_DIM), 2 * HEAD_DIM)


def attention_forward(pairs, queries, keys, values, probs, context, allowed):
    factor = HEAD_DIM ** (-0.5)

    def step(p, carry):
        cols = pair_columns(p)
        scores = dot_nt(both_heads(queries[:, cols]), keys[:, cols]) * factor
        scores = jnp.where(allowed, scores, MASKED)
        exponent = jnp.exp(scores - jnp.max(scores, axis=1, keepdims=True))
        soft = (exponent / jnp.sum(exponent, axis=1, keepdims=True)).astype(BF)
        probs[p] = soft
        context[:, cols] = pick_heads(dot_nn(soft, values[:, cols])).astype(BF)
        return carry

    lax.fori_loop(0, pairs, step, 0)


def slot_choice(own_map, slots, count, part=None):
    rows = own_map.shape[1]
    capacity = slots // count
    reader_iota = lax.broadcasted_iota(jnp.int32, (max(8, count), rows), 0)
    matched = jnp.where(reader_iota == own_map, 1.0, 0.0).astype(F32)
    before = lax.broadcasted_iota(jnp.int32, (rows, rows), 0) < lax.broadcasted_iota(jnp.int32, (rows, rows), 1)
    ranks = dot_nn(matched.astype(BF), jnp.where(before, 1.0, 0.0).astype(BF))
    rank = jnp.sum(matched * ranks, axis=0, keepdims=True).astype(jnp.int32)
    if part is None:
        slot_of = own_map * capacity + rank
    else:
        slots, capacity = slots // 2, capacity // 2
        rank = rank - part * capacity
        slot_of = jnp.where((rank >= 0) & (rank < capacity), own_map * capacity + rank, -1)
    slot_iota = lax.broadcasted_iota(jnp.int32, (slots, rows), 0)
    return jnp.where(slot_iota == slot_of, 1.0, 0.0).astype(BF)


class Gather:
    def __init__(self, here, links, buf, first, depth, placed):
        self.here, self.links, self.buf, self.placed = here, links, buf, placed
        self.mine, self.other = first + here.c, first + 1 - here.c
        self.depth = depth

    def rows(self, at, start, parts):
        size = self.depth // parts
        return pl.ds(pl.multiple_of(at * self.depth + start * size, 16), size)

    def y_half(self, at):
        return self.rows(at, self.here.yy, 2)

    def quarter(self, at, which):
        return self.rows(at, 2 * self.here.yy + which, 4)

    def send(self, where, device, lands, index=None):
        src = self.buf.at[self.mine, where]
        land = self.buf.at[self.mine if index is None else index, lands]
        return self.links.move(src, src, device, land).start()

    def issue(self):
        here = self.here
        for made in self.placed:
            made.wait()
        own = self.y_half(here.w)
        self.from_left = self.send(own, here.to_right, self.y_half(here.left))
        self.from_right = self.send(own, here.to_left, self.y_half(here.right))

    def to_y(self, at):
        return self.send(self.y_half(at), self.here.to_y, self.rows(at, 1 - self.here.yy, 2))

    def forward(self):
        here = self.here
        self.from_left.landed()
        self.far_top = self.send(self.quarter(here.left, 0), here.to_right, self.quarter(here.far, 0))
        self.over_y = [self.to_y(here.left)]
        self.from_right.landed()
        self.far_low = self.send(self.quarter(here.right, 1), here.to_left, self.quarter(here.far, 1))
        self.over_y.append(self.to_y(here.right))

    def complete(self):
        self.far_top.landed()
        self.far_low.landed()
        self.over_y.append(self.to_y(self.here.far))

    def share(self):
        here = self.here
        self.cores = []
        for made, at in zip(self.over_y, (here.left, here.right, here.far)):
            made.landed()
            whole = self.rows(at, 0, 1)
            self.cores.append(self.send(whole, here.to_core, whole, self.other))

    def ready(self):
        for made in self.cores:
            made.landed()


CHUNK = 512


def tall(rows):
    return -(-rows // (2 * CHUNK)) * 2 * CHUNK


def span(at, size):
    return pl.ds(pl.multiple_of(at * size, size), size)


def flip_table(tab, tabt):
    def step(j, carry):
        tabt[:, span(j, CHUNK)] = tab[span(j, CHUNK), :].T
        return carry

    lax.fori_loop(0, tab.shape[0] // CHUNK, step, 0)


def exit_phase(here, links, rows_own, tab, tabt, gt, rb, ids, lens, high, total, stats, stats_tp, stats_wide, coef, weight, acc,
               dx, joint, land_tp, land_far, land_near, swap_out, swap_in, grad_out, vocab, fillers):
    count, g, w, t = here.count, here.g, here.w, here.t
    left, right, far = here.left, here.right, here.far
    to_left, to_right, to_far, to_tp = here.to_left, here.to_right, here.to_far, here.to_tp
    rows, width = rows_own.shape
    half, quarter = rows // 2, rows // 4
    chunks = tab.shape[0] // CHUNK
    scale = float(width) ** (-0.5)
    base = (w * 2 + t) * vocab
    tokens = count * rows

    def block(b):
        return span(b, rows)

    def halved(b, which):
        return pl.ds(pl.multiple_of(b * rows + which * half, half), half)

    def quartered(b, which):
        return pl.ds(pl.multiple_of(b * rows + t * half + which * quarter, quarter), quarter)

    rb[block(w), :] = rows_own[...]
    src = rb.at[halved(w, t)]
    from_left = links.move(src, src, to_right, rb.at[halved(left, t)]).start()
    from_right = links.move(src, src, to_left, rb.at[halved(right, t)]).start()

    def to_other_half(b):
        src = rb.at[halved(b, t)]
        return links.move(src, src, to_tp, rb.at[halved(b, 1 - t)]).start()

    def target_row(cols):
        row = ids[:, cols] - base
        return jnp.where(row < vocab, row, -1)

    def score(b):
        cols = block(b)
        wanted = target_row(cols)
        block_rows = rb[cols, :]

        def step(j, pick):
            at = lax.broadcasted_iota(jnp.int32, (CHUNK, rows), 0) + j * CHUNK
            logits = dot_nt(tab[span(j, CHUNK), :], block_rows) * scale
            logits = jnp.where(at < vocab, logits, MASKED)
            top = jnp.max(logits, axis=0, keepdims=True)
            exponent = jnp.exp(logits - top)
            high[pl.ds(j, 1), cols] = top
            total[pl.ds(j, 1), cols] = jnp.sum(exponent, axis=0, keepdims=True)
            gt[span(j, CHUNK), cols] = exponent.astype(BF)
            return pick + jnp.sum(jnp.where(at == wanted, logits, 0.0), axis=0, keepdims=True)

        pick = lax.fori_loop(0, chunks, step, jnp.zeros((1, rows), F32), unroll=True)
        tops = high[:, cols]
        top = jnp.max(tops, axis=0, keepdims=True)
        stats[0:1, cols] = top
        stats[1:2, cols] = jnp.sum(total[:, cols] * jnp.exp(tops - top), axis=0, keepdims=True)
        stats[2:3, cols] = pick

    score(w)
    from_left.landed()
    src = rb.at[quartered(left, 0)]
    far_top = links.move(src, src, to_right, rb.at[quartered(far, 0)]).start()
    left_rest = to_other_half(left)
    from_right.landed()
    src = rb.at[quartered(right, 1)]
    far_low = links.move(src, src, to_left, rb.at[quartered(far, 1)]).start()
    right_rest = to_other_half(right)
    left_rest.landed()
    score(left)
    far_top.landed()
    far_low.landed()
    far_rest = to_other_half(far)
    right_rest.landed()
    score(right)
    far_rest.landed()
    score(far)

    def merged_stats(parts):
        top = parts[0][0:1]
        for part in parts[1:]:
            top = jnp.maximum(top, part[0:1])
        mass = sum(part[1:2] * jnp.exp(part[0:1] - top) for part in parts)
        pick = sum(part[2:3] for part in parts)
        return top, mass, pick

    swap = links.move(stats, stats_tp, to_tp, stats_tp).start()
    lengths = [lens[k] for k in range(lens.shape[0])]
    tokens_all = lengths[0]
    for length in lengths[1:]:
        tokens_all = tokens_all + length
    place = lax.broadcasted_iota(jnp.int32, (1, rows), 1)
    for b in range(count):
        inside = jnp.where(place < lens[g * count + b], 1.0, 0.0).astype(F32)
        weight[0:1, b * rows : (b + 1) * rows] = inside / tokens_all.astype(F32)
    swap.landed()
    mine, other = stats[...], stats_tp[...]
    top, mass, pick = merged_stats([mine, other])
    mine_wide = stats_wide.at[w]
    mine_wide[0:1, :] = top
    mine_wide[1:2, :] = mass
    mine_wide[2:3, :] = pick
    spreads = [
        links.move(mine_wide, mine_wide, device, stats_wide.at[at]).start()
        for device, at in ((to_left, right), (to_right, left), (to_far, far))
    ]
    for made in spreads:
        made.landed()
    top, mass, pick = merged_stats([stats_wide[b] for b in range(count)])
    log_total = top + jnp.log(mass)
    all_weight = weight[0:1, :]
    coef[...] = jnp.exp(high[...] - log_total) * all_weight
    stats_tp[3:4, :] = (log_total - pick) * all_weight
    loss = jnp.sum(stats_tp[3:4, block(w)], axis=1, keepdims=True)

    def row_grads(b):
        cols = block(b)
        wanted = target_row(cols)
        own_weight = weight[0:1, cols]
        acc[...] = jnp.zeros_like(acc)

        def step(j, carry):
            at = lax.broadcasted_iota(jnp.int32, (CHUNK, rows), 0) + j * CHUNK
            grad = gt[span(j, CHUNK), cols].astype(F32) * coef[pl.ds(j, 1), cols]
            grad = (grad - jnp.where(at == wanted, own_weight, 0.0)).astype(BF)
            gt[span(j, CHUNK), cols] = grad
            acc[...] += dot_nn(tabt[:, span(j, CHUNK)], grad)
            return carry

        lax.fori_loop(0, chunks, step, 0, unroll=True)
        return (acc[...] * scale).astype(BF).T

    own_half, other_half = (span(which, half) for which in (t, 1 - t))

    def start_block(slot, b):
        dx[slot] = row_grads(b)
        return links.move(dx.at[slot, other_half], land_tp.at[slot], to_tp, land_tp.at[slot]).start()

    def join_block(slot, made):
        made.landed()
        joint[slot] = (dx[slot, own_half].astype(F32) + land_tp[slot].astype(F32)).astype(BF)

    parts = [pl.ds(which * quarter, quarter) for which in range(2)]

    def near(slot, which, side, device):
        where = parts[which]
        return links.move(joint.at[slot, where], land_near.at[side, where], device, land_near.at[side, where]).start()

    made_far = start_block(0, far)
    made_right = start_block(1, right)
    join_block(0, made_far)
    far_moves = [
        links.move(joint.at[0, parts[which]], land_far.at[which], device, land_far.at[which]).start()
        for which, device in enumerate((to_right, to_left))
    ]
    made_left = start_block(2, left)
    join_block(1, made_right)
    right_low = near(1, 1, 0, to_right)
    made_own = start_block(3, w)
    fillers[0]()
    join_block(2, made_left)
    left_top = near(2, 0, 1, to_left)
    near_late = []
    for which, slot, device in ((0, 1, to_right), (1, 2, to_left)):
        far_moves[which].landed()
        where = parts[which]
        joint[slot, where] = (joint[slot, where].astype(F32) + land_far[which].astype(F32)).astype(BF)
        near_late.append(near(slot, which, which, device))
    fillers[1]()
    join_block(3, made_own)
    for made in [right_low, left_top] + near_late:
        made.landed()
    swap_out[...] = (joint[3].astype(F32) + land_near[0].astype(F32) + land_near[1].astype(F32)).astype(BF)
    swap = links.move(swap_out, swap_in, to_tp, swap_in).start()
    grad_out[own_half, :] = swap_out[...].astype(F32)
    swap.landed()
    grad_out[other_half, :] = swap_in[...].astype(F32)
    return loss


class TableGrad:
    def __init__(self, here, links, copies, tab, gt, rb, land_core, out):
        self.here, self.links, self.copies = here, links, copies
        self.tab, self.gt, self.rb, self.land_core, self.out = tab, gt, rb, land_core, out
        self.pieces = tab.shape[0] // (2 * CHUNK)
        self.scale = float(tab.shape[1]) ** (-0.5)
        self.cores = []

    def rows(self, owner, i):
        return pl.ds(pl.multiple_of((owner * self.pieces + i) * CHUNK, CHUNK), CHUNK)

    def product(self, where):
        return dot_nn(self.gt[where, :], self.rb[...]) * self.scale

    def first_half(self):
        c = self.here.c
        for i in range(self.pieces):
            where = self.rows(1 - c, i)
            self.tab[where, :] = self.product(where).astype(BF)
            land = self.land_core.at[pl.ds(i * CHUNK, CHUNK)]
            self.cores.append(self.links.move(self.tab.at[where], land, self.here.to_core, land).start())

    def second_half(self):
        c = self.here.c
        for i in range(self.pieces):
            where = self.rows(c, i)
            mine = self.product(where)
            self.cores[i].landed()
            self.tab[where, :] = (mine + self.land_core[i * CHUNK : (i + 1) * CHUNK, :].astype(F32)).astype(BF)
            self.copies.save(self.tab.at[where], self.out.at[pl.ds(i * CHUNK, CHUNK)])


def front_kernel(
    count, vocab, x_ref, mem_ref, map_ref, len_ref, gs_ref, gc_ref, gf_ref, ge_ref, ids,
    q_in, k_in, v_in, so_in, cq_in, ck_in, cv_in, co_in, ga_in, up_in, dn_in, table,
    block_o, one_o, two_o, three_o, q_o, k_o, v_o, cq_o, mk_o, mv_o, sc_o, cc_o, ps_o, pc_o,
    ga_o, up_o, sel_o, wa_o, wgu_o, wd_o, gain_o, grad_o, loss_o, half_o,
    wa, wgu, wd, gains, slots, packed, part_out, part_in, valid_slot,
    block, one, two, three, q, k, v, cq, mk, mv, sc, cc, ps, pc, ga, up, gain_sum, exit_rows,
    tab, tabt, gt, rb, high_v, total, stats, stats_tp, stats_wide, coef, weight, acc, dx, joint, land_tp, land_far, land_near,
    swap_out, swap_in, land_core,
    send_sems, recv_sems, copy_sems,
):
    here = position(count)
    g, w, t = here.g, here.w, here.t
    left, right, far = here.left, here.right, here.far
    to_left, to_right, to_far, to_tp = here.to_left, here.to_right, here.to_far, here.to_tp
    rows = x_ref.shape[0]
    links, copies = Links(send_sems, recv_sems), Copies(copy_sems)
    depth = q_in.shape[0]
    wide_cols = dn_in.shape[1] // 2

    own = pl.ds(pl.multiple_of(w * depth, 16), depth)
    order = (q_in, k_in, v_in, so_in, ck_in, cv_in, cq_in, co_in)
    weights = []
    for j in range(4):
        placed = [copies.start(order[2 * j + e], wa.at[2 * j + e, own]) for e in range(2)]
        weights.append(Gather(here, links, wa, 2 * j, depth, placed))
    for f in range(2):
        cols = pl.ds(f * wide_cols, wide_cols)
        placed = [copies.start(ref.at[:, cols], wgu.at[2 * f + e, own]) for e, ref in enumerate((ga_in, up_in))]
        weights.append(Gather(here, links, wgu, 2 * f, depth, placed))
    placed = [copies.start(dn_in.at[:, pl.ds(e * wide_cols, wide_cols)], wd.at[e, own]) for e in range(2)]
    weights.append(Gather(here, links, wd, 0, depth, placed))

    gain_sum[...] = jnp.zeros_like(gain_sum)
    for n, ref in enumerate((gs_ref, gc_ref, gf_ref, ge_ref)):
        gain_sum[n : n + 1, 0:depth] = ref[...].astype(F32).reshape(1, depth)
    gains[w] = pltpu.roll(gain_sum[...], w * depth, 1)
    table_load = copies.start(table, tab.at[pl.ds(0, vocab)])
    tab[vocab:, :] = jnp.zeros((tab.shape[0] - vocab, tab.shape[1]), BF)
    greet([to_left, to_right, to_far, here.to_core, here.to_y, to_tp])
    gain_moves = [
        links.move(gains.at[w], gains.at[w], device, gains.at[at]).start()
        for device, at in ((to_left, right), (to_right, left), (to_far, far))
    ]
    for first in weights[:3]:
        first.issue()

    capacity = slots.shape[0] // count
    choose = slot_choice(map_ref[:, pl.ds(pl.multiple_of(w * rows, rows), rows)], slots.shape[0], count)
    packed[...] = dot_nn(choose, mem_ref[...]).astype(BF)

    def slot_rows(at, which):
        return pl.ds(pl.multiple_of(at * capacity + which * (capacity // 2), 16), capacity // 2)

    own_slots = pl.ds(pl.multiple_of(w * capacity, 16), capacity)
    slots[own_slots, :] = packed[own_slots, :]
    weights[0].forward()
    weights[3].issue()
    for made in gain_moves:
        made.landed()
    total_gain = gains[0]
    for at in range(1, count):
        total_gain = total_gain + gains[at]
    gain_sum[...] = total_gain
    hidden = x_ref[...].astype(F32)
    norm_self = rms_rows(hidden, gain_sum[0:1, :])
    weights[1].forward()
    weights[0].complete()
    slot_moves = [
        links.move(packed.at[slot_rows(to, t)], slots.at[slot_rows(w, t)], device, slots.at[slot_rows(at, t)]).start()
        for device, to, at in ((to_left, left, right), (to_right, right, left), (to_far, far, far))
    ]
    weights[2].forward()
    weights[0].share()
    weights[1].complete()
    weights[1].share()
    weights[4].issue()
    weights[0].ready()
    q[...] = dot_nn(norm_self, wa[0]).astype(BF)
    k[...] = dot_nn(norm_self, wa[1]).astype(BF)
    weights[2].complete()
    weights[1].ready()
    v[...] = dot_nn(norm_self, wa[2]).astype(BF)
    weights[3].forward()
    weights[2].share()
    weights[5].issue()
    weights[3].complete()
    slot_fills = []
    for made, at in zip(slot_moves, (right, left, far)):
        made.landed()
        src = slots.at[slot_rows(at, t)]
        slot_fills.append(links.move(src, src, to_tp, slots.at[slot_rows(at, 1 - t)]).start())
    length = len_ref[g * count + w]
    query_at = lax.broadcasted_iota(jnp.int32, (2 * rows, rows), 0)
    query_at = jnp.where(query_at >= rows, query_at - rows, query_at)
    key_at = lax.broadcasted_iota(jnp.int32, (2 * rows, rows), 1)
    allowed_self = (key_at <= query_at) & (key_at < length)
    pairs = q.shape[1] // (2 * HEAD_DIM)
    attention_forward(pairs, q, k, v, ps, sc, allowed_self)

    def exchange_start(n):
        return links.move(part_out.at[n], part_in.at[n], to_tp, part_in.at[n]).start()

    def exchanged(n, made):
        made.landed()
        return part_out[n].astype(F32) + part_in[n].astype(F32)

    part_out[0] = dot_nt(sc[...], wa[3]).astype(BF)
    swap = exchange_start(0)
    weights[3].share()
    weights[4].forward()
    weights[6].issue()
    for made in slot_fills:
        made.landed()
    place = lax.broadcasted_iota(jnp.int32, (1, capacity), 1).astype(F32)
    for b in range(count):
        reads = jnp.sum(jnp.where(map_ref[:, b * rows : (b + 1) * rows] == w, 1.0, 0.0), axis=1, keepdims=True)
        valid_slot[0:1, b * capacity : (b + 1) * capacity] = jnp.where(place < reads, 1.0, 0.0)
    weights[2].ready()
    mk[...] = dot_nn(slots[...], wa[4]).astype(BF)
    mv[...] = dot_nn(slots[...], wa[5]).astype(BF)
    weights[4].complete()
    weights[5].forward()
    allowed_cross = jnp.broadcast_to(valid_slot[0:1, :], (2 * rows, slots.shape[0])) > 0.5
    one[...] = hidden + exchanged(0, swap)
    norm_cross = rms_rows(one[...], gain_sum[1:2, :])
    weights[3].ready()
    cq[...] = dot_nn(norm_cross, wa[6]).astype(BF)
    weights[4].share()
    weights[5].complete()
    weights[6].forward()
    attention_forward(pairs, cq, mk, mv, pc, cc, allowed_cross)
    part_out[1] = dot_nt(cc[...], wa[7]).astype(BF)
    swap = exchange_start(1)
    weights[5].share()
    weights[6].complete()
    weights[6].share()
    table_load.wait()
    flip_table(tab, tabt)
    copies.save(wa, wa_o)
    for src, dst in (
        (q, q_o), (k, k_o), (v, v_o), (sc, sc_o), (ps, ps_o), (mk, mk_o), (mv, mv_o), (cq, cq_o), (cc, cc_o), (pc, pc_o),
        (slots, sel_o), (one, one_o), (gain_sum, gain_o),
    ):
        copies.save(src, dst)
    two[...] = one[...] + exchanged(1, swap)
    copies.save(two, two_o)
    norm_ff = rms_rows(two[...], gain_sum[2:3, :])
    low, high = pl.ds(0, wide_cols), pl.ds(wide_cols, wide_cols)
    for f, cols in ((0, low), (1, high)):
        weights[4 + f].ready()
        ga[:, cols] = dot_nn(norm_ff, wgu[2 * f]).astype(BF)
        up[:, cols] = dot_nn(norm_ff, wgu[2 * f + 1]).astype(BF)
    copies.save(wgu, wgu_o)
    copies.save(ga, ga_o)
    copies.save(up, up_o)
    ff_hidden = (smooth_gate(ga[...].astype(F32)) * up[...].astype(F32)).astype(BF)
    weights[6].ready()
    copies.save(wd, wd_o)
    part_out[2] = (
        dot_nt(ff_hidden[:, :wide_cols], wd[0]) + dot_nt(ff_hidden[:, wide_cols:], wd[1])
    ).astype(BF)
    swap = exchange_start(2)
    three[...] = two[...] + exchanged(2, swap)
    block[...] = three[...].astype(BF)
    exit_rows[...] = rms_rows(three[...], gain_sum[3:4, :])
    copies.save(three, three_o)
    copies.save(block, block_o)
    grads = TableGrad(here, links, copies, tab, gt, rb, land_core, half_o)
    loss = exit_phase(
        here, links, exit_rows, tab, tabt, gt, rb, ids, len_ref, high_v, total, stats, stats_tp, stats_wide, coef, weight, acc,
        dx, joint, land_tp, land_far, land_near, swap_out, swap_in, grad_o, vocab, (grads.first_half, grads.second_half),
    )
    loss_o[...] = jnp.broadcast_to(loss, loss_o.shape)
    links.finish()
    copies.finish()


def front(count, layer_input, memory, group_map, lengths, gain_parts, ids, weights, table):
    rows, width = layer_input.shape
    vocab = table.shape[0]
    heads, units = weights[0].shape[1], weights[8].shape[1]
    slots = count * max(2, 2 * rows // count)
    pairs = heads // (2 * HEAD_DIM)
    kept = [
        ((rows, width), BF), ((rows, width), F32), ((rows, width), F32), ((rows, width), F32),
        ((rows, heads), BF), ((rows, heads), BF), ((rows, heads), BF), ((rows, heads), BF),
        ((slots, heads), BF), ((slots, heads), BF), ((rows, heads), BF), ((rows, heads), BF),
        ((pairs, 2 * rows, rows), BF), ((pairs, 2 * rows, slots), BF),
        ((rows, units), BF), ((rows, units), BF), ((slots, width), BF),
        ((8, width, heads), BF), ((4, width, units // 2), BF), ((2, width, units // 2), BF), ((8, width), F32),
    ]
    high = tall(vocab)
    chunks, tokens = high // CHUNK, rows * count
    vmem, hbm, smem = (pl.BlockSpec(memory_space=space) for space in (pltpu.VMEM, pl.ANY, pltpu.SMEM))
    scratch = [
        ((8, width, heads), BF), ((4, width, units // 2), BF), ((2, width, units // 2), BF), ((count, 8, width), F32),
        ((slots, width), BF), ((slots, width), BF), ((3, rows, width), BF), ((3, rows, width), BF), ((8, slots), F32),
    ]
    scratch += kept[:16]
    scratch += [
        ((8, width), F32), ((rows, width), BF),
        ((high, width), BF), ((width, high), BF), ((high, tokens), BF), ((tokens, width), BF), ((chunks, tokens), F32),
        ((chunks, tokens), F32), ((8, tokens), F32), ((8, tokens), F32), ((count, 8, tokens), F32), ((chunks, tokens), F32),
        ((8, tokens), F32), ((width, rows), F32), ((4, rows, width), BF), ((4, rows // 2, width), BF), ((4, rows // 2, width), BF),
        ((2, rows // 4, width), BF), ((2, rows // 2, width), BF), ((rows // 2, width), BF), ((rows // 2, width), BF),
        ((high // 2, width), BF),
    ]
    results = kept + [((rows, width), F32), ((8, 128), F32), ((high // 2, width), BF)]
    return pl.pallas_call(
        functools.partial(front_kernel, count, vocab),
        out_shape=[jax.ShapeDtypeStruct(shape, kind) for shape, kind in results],
        in_specs=[vmem, vmem, vmem, smem] + [vmem] * 5 + [hbm] * 12,
        out_specs=[hbm] * len(kept) + [vmem, vmem, hbm],
        scratch_shapes=[pltpu.VMEM(shape, kind) for shape, kind in scratch]
        + [pltpu.SemaphoreType.DMA((128,)), pltpu.SemaphoreType.DMA((128,)), pltpu.SemaphoreType.DMA((48,))],
        compiler_params=pltpu.CompilerParams(collective_id=0, has_side_effects=True, vmem_limit_bytes=VMEM_BYTES),
        name="forward_and_exit",
    )(layer_input, memory, group_map, lengths, *gain_parts, ids, *weights, table)


GELU_SCALE = 0.7978845608028654
GELU_CUBE = 0.044715


def norm_back(values, gain, grad):
    factor = lax.rsqrt(jnp.mean(values * values, axis=1, keepdims=True) + EPSILON)
    unit = values * factor
    scaled = grad * gain
    inner = jnp.mean(scaled * values, axis=1, keepdims=True)
    return jnp.sum(grad * unit, axis=0, keepdims=True), factor * scaled - unit * (factor * factor * inner)


def attention_backward(pairs, queries, keys, values, probs, context_grad, query_grad, key_grad, value_grad):
    factor = HEAD_DIM ** (-0.5)

    def step(p, carry):
        cols = pair_columns(p)
        grad = both_heads(context_grad[:, cols])
        soft = probs[p]
        soft_float = soft.astype(F32)
        soft_grad = dot_nt(grad, values[:, cols])
        inner = jnp.sum(soft_float * soft_grad, axis=1, keepdims=True)
        score_grad = (soft_float * (soft_grad - inner)).astype(BF)
        query_grad[:, cols] = (pick_heads(dot_nn(score_grad, keys[:, cols])) * factor).astype(BF)
        key_grad[:, cols] = (dot_tn(score_grad, both_heads(queries[:, cols])) * factor).astype(BF)
        value_grad[:, cols] = dot_tn(soft, grad).astype(BF)
        return carry

    lax.fori_loop(0, pairs, step, 0)


class WeightGrad:
    def __init__(self, here, links, copies, grads, first, depth, land_core, land_far, land_near, land_y, mine_out, out):
        self.here, self.links, self.copies = here, links, copies
        self.grads, self.mine, self.other = grads, first + here.c, first + 1 - here.c
        self.depth, self.half = depth, depth // 2
        self.land_core, self.land_far, self.land_near, self.land_y = land_core, land_far, land_near, land_y
        self.mine_out, self.out = mine_out, out

    def whole(self, at):
        return pl.ds(pl.multiple_of(at * self.depth, 16), self.depth)

    def part(self, at, which):
        return pl.ds(pl.multiple_of(at * self.depth + which * self.half, 16), self.half)

    def pair(self):
        self.core = self.links.move(
            self.grads.at[self.other], self.land_core, self.here.to_core, self.land_core
        ).start()

    def near(self, where, side, which, device):
        rows = pl.ds(which * self.half, self.half)
        return self.links.move(
            self.grads.at[self.mine, where], self.land_near.at[side, rows], device, self.land_near.at[side, rows]
        ).start()

    def add_core(self, where):
        self.grads[self.mine, where] = (
            self.grads[self.mine, where].astype(F32) + self.land_core[where].astype(F32)
        ).astype(BF)

    def ring(self):
        here = self.here
        self.core.landed()
        for at in (here.far, here.right, here.left):
            self.add_core(self.whole(at))
            if at is here.far:
                self.far = [
                    self.links.move(
                        self.grads.at[self.mine, self.part(at, e)], self.land_far.at[e], way, self.land_far.at[e]
                    ).start()
                    for e, way in enumerate((here.to_right, here.to_left))
                ]
        self.early = [
            self.near(self.part(here.right, 1), 0, 1, here.to_right),
            self.near(self.part(here.left, 0), 1, 0, here.to_left),
        ]
        self.add_core(self.whole(here.w))

    def pass_on(self):
        here = self.here
        self.late = []
        for e, side, way in ((0, here.right, here.to_right), (1, here.left, here.to_left)):
            self.far[e].landed()
            where = self.part(side, e)
            self.grads[self.mine, where] = (
                self.grads[self.mine, where].astype(F32) + self.land_far[e].astype(F32)
            ).astype(BF)
            self.late.append(self.near(where, e, e, way))

    def across(self):
        for made in self.early + self.late:
            made.landed()
        where = self.whole(self.here.w)
        self.mine_out[0] = (
            self.grads[self.mine, where].astype(F32) + self.land_near[0].astype(F32) + self.land_near[1].astype(F32)
        ).astype(BF)
        self.y = self.links.move(self.mine_out.at[0], self.land_y, self.here.to_y, self.land_y).start()

    def settle(self):
        self.y.landed()
        self.mine_out[1] = (self.mine_out[0].astype(F32) + self.land_y[...].astype(F32)).astype(BF)
        src = self.mine_out.at[1]
        self.copies.save(src, self.out.at[self.mine])
        self.share = self.links.move(
            src, self.out.at[self.mine], self.here.to_core, self.out.at[self.other]
        ).start()

    def done(self):
        self.share.landed()


def backward_kernel(
    count,
    lens, map_ref, x_h, og_h, eg_h, loss_h, one_h, two_h, three_h, q_h, k_h, v_h, cq_h, mk_h, mv_h, sc_h, cc_h, ps_h, pc_h,
    ga_h, up_h, sel_h, wa_h, wgu_h, wd_h, gain_h, half_h,
    in_o, mem_o, small_o, ga8_o, ggu_o, gd_o, table_o,
    x, og, eg, loss, one, two, three, q, k, v, cq, mk, mv, sc, cc, ps, pc, ga, up, sel, wa, wgu, wd, gain, tab, land_t,
    part_out, part_in, grad, dq, dk, dv, dmk, dmv, dctx, gate_grad, up_grad, ff_hidden,
    g8, ggu, gd, lc8, lcg, lcd, lf8, lfg, lfd, ln8, lng, lnd, ly8, lyg, lyd, mo8, mog, mod,
    back_slots, land_slots, got_slots, small, small_wide, small_land,
    send_sems, recv_sems, copy_sems,
):
    here = position(count)
    links, copies = Links(send_sems, recv_sems), Copies(copy_sems)
    w, t, c = here.w, here.t, here.c
    to_left, to_right, to_far, to_tp = (here.to_left, here.to_right, here.to_far, here.to_tp)
    loads = {}
    for src, dst in (
        (gain_h, gain), (three_h, three), (eg_h, eg), (og_h, og), (ga_h, ga), (up_h, up), (wd_h, wd), (half_h, tab), (wgu_h, wgu),
        (two_h, two), (wa_h, wa), (cc_h, cc), (pc_h, pc), (cq_h, cq), (mk_h, mk), (mv_h, mv), (sel_h, sel), (one_h, one),
        (sc_h, sc), (ps_h, ps), (q_h, q), (k_h, k), (v_h, v), (x_h, x), (loss_h, loss),
    ):
        loads[id(dst)] = copies.start(src, dst)

    def need(*refs):
        for ref in refs:
            loads.pop(id(ref)).wait()

    greet([to_left, to_right, to_far, here.to_core, here.to_y, to_tp])

    pieces = tab.shape[0] // CHUNK
    need(tab)
    crossing = [
        links.move(tab.at[pl.ds(i * CHUNK, CHUNK)], land_t.at[pl.ds(i * CHUNK, CHUNK)], here.to_y, land_t.at[pl.ds(i * CHUNK, CHUNK)]).start()
        for i in range(pieces)
    ]
    shares = []

    def settle_table(i):
        piece = pl.ds(i * CHUNK, CHUNK)
        crossing[i].landed()
        crossing[i].sent()
        tab[piece, :] = (tab[piece, :].astype(F32) + land_t[piece, :].astype(F32)).astype(BF)

        def rows(owner):
            return pl.ds(pl.multiple_of((owner * pieces + i) * CHUNK, CHUNK), CHUNK)

        copies.save(tab.at[piece], table_o.at[rows(c)])
        shares.append(
            links.move(tab.at[piece], table_o.at[rows(c)], here.to_core, table_o.at[rows(1 - c)]).start()
        )

    depth = g8.shape[1] // count

    def weight_pair(i):
        if i < 4:
            return WeightGrad(here, links, copies, g8, 2 * i, depth, lc8.at[i], lf8.at[i], ln8.at[i], ly8.at[i], mo8.at[i], ga8_o)
        if i == 4:
            return WeightGrad(here, links, copies, ggu, 0, depth, lcg, lfg, lng, lyg, mog, ggu_o)
        return WeightGrad(here, links, copies, gd, 0, depth, lcd, lfd, lnd, lyd, mod, gd_o)

    pair = [weight_pair(i) for i in range(6)]

    def exchange_start(n):
        return links.move(part_out.at[n], part_in.at[n], to_tp, part_in.at[n]).start()

    def exchanged(n, made):
        made.landed()
        return part_out[n].astype(F32) + part_in[n].astype(F32)

    small[...] = jnp.zeros_like(small)
    need(gain, three, eg, og)
    gain_row, back = norm_back(three[...], gain[3:4, :], eg[...])
    small[3:4, :] = gain_row
    grad[...] = og[...].astype(F32) + back
    branch = grad[...].astype(BF)
    need(ga, up, wd)
    units = wd.shape[2]
    for e in range(2):
        cols = slice(e * units, (e + 1) * units)
        act = ga[:, cols].astype(F32)
        up_act = up[:, cols].astype(F32)
        square = act * act
        bend = jnp.tanh(GELU_SCALE * (act + GELU_CUBE * act * square))
        gate = 0.5 * act * (1.0 + bend)
        slope = 0.5 * (1.0 + bend) + 0.5 * act * (1.0 - bend * bend) * (GELU_SCALE * (1.0 + 3.0 * GELU_CUBE * square))
        hidden_grad = dot_nn(branch, wd[e])
        gate_grad[:, cols] = (hidden_grad * up_act * slope).astype(BF)
        up_grad[:, cols] = (hidden_grad * gate).astype(BF)
        ff_hidden[:, cols] = (gate * up_act).astype(BF)
    need(wgu)
    total = dot_nt(gate_grad[:, :units], wgu[0]) + dot_nt(up_grad[:, :units], wgu[1])
    total += dot_nt(gate_grad[:, units:], wgu[2]) + dot_nt(up_grad[:, units:], wgu[3])
    part_out[0] = total.astype(BF)
    swap = exchange_start(0)
    need(two)
    norm_t = rms_rows(two[...], gain[2:3, :]).T
    ggu[0] = dot_nn(norm_t, gate_grad[...]).astype(BF)
    ggu[1] = dot_nn(norm_t, up_grad[...]).astype(BF)
    pair[4].pair()
    branch_rows = branch.T
    for e in range(2):
        gd[e] = dot_nn(branch_rows, ff_hidden[:, e * units : (e + 1) * units]).astype(BF)
    pair[5].pair()
    pair[4].ring()
    gain_row, back = norm_back(two[...], gain[2:3, :], exchanged(0, swap))
    small[2:3, :] = gain_row
    grad[...] += back

    branch = grad[...].astype(BF)
    need(wa, cc, pc, cq, mk, mv, sel)
    dctx[...] = dot_nn(branch, wa[7]).astype(BF)
    pairs = dctx.shape[1] // (2 * HEAD_DIM)
    attention_backward(pairs, cq, mk, mv, pc, dctx, dq, dmk, dmv)
    part_out[1] = dot_nt(dq[...], wa[6]).astype(BF)
    swap = exchange_start(1)
    pair[5].ring()
    pair[4].pass_on()
    need(one)
    slots_grad = (dot_nt(dmk[...], wa[4]) + dot_nt(dmv[...], wa[5])).astype(BF)
    capacity = slots_grad.shape[0] // count
    half_slots = capacity // 2
    for b in range(count):
        for e in range(2):
            start = b * capacity + e * half_slots
            back_slots[e, b * half_slots : (b + 1) * half_slots] = slots_grad[start : start + half_slots]
    mem_swap = links.move(back_slots.at[1 - t], land_slots, to_tp, land_slots).start()

    def slot_rows(at):
        return pl.ds(pl.multiple_of(at * half_slots, 16), half_slots)

    g8[7] = dot_nn(branch.T, cc[...]).astype(BF)
    norm_t = rms_rows(one[...], gain[1:2, :]).T
    g8[6] = dot_nn(norm_t, dq[...]).astype(BF)
    pair[3].pair()
    slots_t = sel[...].T
    g8[4] = dot_nn(slots_t, dmk[...]).astype(BF)
    g8[5] = dot_nn(slots_t, dmv[...]).astype(BF)
    pair[2].pair()
    pair[5].pass_on()
    pair[3].ring()
    pair[2].ring()
    mem_swap.landed()
    back_slots[t] = (back_slots[t].astype(F32) + land_slots[...].astype(F32)).astype(BF)
    returns = [
        links.move(back_slots.at[t, slot_rows(to)], got_slots.at[slot_rows(w)], device, got_slots.at[slot_rows(at)]).start()
        for device, to, at in ((to_left, here.left, here.right), (to_right, here.right, here.left), (to_far, here.far, here.far))
    ]
    got_slots[slot_rows(w), :] = back_slots[t, slot_rows(w), :]
    gain_row, back = norm_back(one[...], gain[1:2, :], exchanged(1, swap))
    small[1:2, :] = gain_row
    grad[...] += back

    branch = grad[...].astype(BF)
    need(sc, ps, q, k, v, x)
    dctx[...] = dot_nn(branch, wa[3]).astype(BF)
    attention_backward(pairs, q, k, v, ps, dctx, dq, dk, dv)
    part_out[2] = (dot_nt(dq[...], wa[0]) + dot_nt(dk[...], wa[1]) + dot_nt(dv[...], wa[2])).astype(BF)
    swap = exchange_start(2)
    hidden = x[...].astype(F32)
    norm_t = rms_rows(hidden, gain[0:1, :]).T
    g8[0] = dot_nn(norm_t, dq[...]).astype(BF)
    g8[1] = dot_nn(norm_t, dk[...]).astype(BF)
    pair[0].pair()
    g8[2] = dot_nn(norm_t, dv[...]).astype(BF)
    g8[3] = dot_nn(branch.T, sc[...]).astype(BF)
    pair[1].pair()
    pair[3].pass_on()
    pair[2].pass_on()
    pair[0].ring()
    pair[1].ring()
    pair[4].across()
    pair[5].across()
    for made in returns:
        made.landed()
    rows = x.shape[0]
    choose = slot_choice(map_ref[:, pl.ds(pl.multiple_of(w * rows, rows), rows)], slots_grad.shape[0], count, t)
    part_out[3] = dot_tn(choose, got_slots[...]).astype(BF)
    memory_swap = exchange_start(3)
    gain_row, back = norm_back(hidden, gain[0:1, :], exchanged(2, swap))
    small[0:1, :] = gain_row
    grad[...] += back
    copies.save(grad, in_o)
    need(loss)
    small[4:5, 0:128] = loss[0:1, :]

    small_wide[w] = small[...]
    sums = [
        links.move(small, small_wide.at[w], device, small_wide.at[at]).start()
        for device, at in ((to_left, here.right), (to_right, here.left), (to_far, here.far))
    ]
    pair[0].pass_on()
    pair[1].pass_on()
    pair[3].across()
    pair[2].across()
    for made in sums:
        made.landed()
    total = small_wide[0]
    for b in range(1, count):
        total = total + small_wide[b]
    for n, way in enumerate((here.to_core, here.to_y)):
        small_land[2 * n] = total
        made = links.move(small_land.at[2 * n], small_land.at[2 * n + 1], way, small_land.at[2 * n + 1]).start()
        if n == 0:
            pair[0].across()
            pair[1].across()
        made.landed()
        total = total + small_land[2 * n + 1]
    small_o[...] = total
    mem_o[...] = exchanged(3, memory_swap)
    for i in range(pieces):
        settle_table(i)
    for i in (4, 5, 3, 2, 0, 1):
        pair[i].settle()
    for i in (4, 5, 3, 2, 0, 1):
        pair[i].done()
    for made in shares:
        made.landed()
    links.finish_rest(crossing)
    copies.finish()


def backward_layer(count, lengths, group_map, kept, table_half):
    (layer_input, out_grad, exit_rows_grad, loss_part, one, two, three, q, k, v, cq, mk, mv, sc, cc, ps, pc, ga, up, sel,
     wa, wgu, wd, gains) = kept
    rows, width = layer_input.shape
    heads, units = wa.shape[2], ga.shape[1]
    slots, depth = sel.shape[0], width // count
    half, narrow = depth // 2, units // 2
    piece_rows = table_half.shape[0]
    high = 2 * piece_rows
    vmem, hbm = pl.BlockSpec(memory_space=pltpu.VMEM), pl.BlockSpec(memory_space=pl.ANY)

    def three_kinds(rows_of, lead=()):
        return [
            pltpu.VMEM((4,) + lead + (rows_of, heads), BF), pltpu.VMEM(lead + (rows_of, units), BF),
            pltpu.VMEM(lead + (rows_of, narrow), BF),
        ]

    scratch = [pltpu.VMEM(value.shape, value.dtype) for value in kept]
    scratch += [pltpu.VMEM((piece_rows, width), BF), pltpu.VMEM((piece_rows, width), BF)]
    scratch += [
        pltpu.VMEM((4, rows, width), BF), pltpu.VMEM((4, rows, width), BF), pltpu.VMEM((rows, width), F32),
        pltpu.VMEM((rows, heads), BF), pltpu.VMEM((rows, heads), BF), pltpu.VMEM((rows, heads), BF),
        pltpu.VMEM((slots, heads), BF), pltpu.VMEM((slots, heads), BF), pltpu.VMEM((rows, heads), BF),
        pltpu.VMEM((rows, units), BF), pltpu.VMEM((rows, units), BF), pltpu.VMEM((rows, units), BF),
        pltpu.VMEM((8, width, heads), BF), pltpu.VMEM((2, width, units), BF), pltpu.VMEM((2, width, narrow), BF),
    ]
    scratch += three_kinds(width)
    scratch += three_kinds(half, (2,))
    scratch += three_kinds(depth, (2,))
    scratch += three_kinds(depth)
    scratch += three_kinds(depth, (2,))
    scratch += [
        pltpu.VMEM((2, slots // 2, width), BF), pltpu.VMEM((slots // 2, width), BF), pltpu.VMEM((slots // 2, width), BF), pltpu.VMEM((8, width), F32),
        pltpu.VMEM((count, 8, width), F32), pltpu.VMEM((4, 8, width), F32),
        pltpu.SemaphoreType.DMA((80,)), pltpu.SemaphoreType.DMA((80,)), pltpu.SemaphoreType.DMA((48,)),
    ]
    return pl.pallas_call(
        functools.partial(backward_kernel, count),
        out_shape=[
            jax.ShapeDtypeStruct((rows, width), F32), jax.ShapeDtypeStruct((rows, width), F32),
            jax.ShapeDtypeStruct((8, width), F32), jax.ShapeDtypeStruct((8, depth, heads), BF),
            jax.ShapeDtypeStruct((2, depth, units), BF), jax.ShapeDtypeStruct((2, depth, narrow), BF),
            jax.ShapeDtypeStruct((high, width), BF),
        ],
        in_specs=[pl.BlockSpec(memory_space=pltpu.SMEM), vmem] + [hbm] * (len(kept) + 1),
        out_specs=[hbm, vmem, vmem, hbm, hbm, hbm, hbm],
        scratch_shapes=scratch,
        compiler_params=pltpu.CompilerParams(
            collective_id=2, has_side_effects=True, vmem_limit_bytes=VMEM_BYTES
        ),
        name="backward_layer",
    )(lengths, group_map, *kept, table_half)


def finish_kernel(
    vocab, attn_ref, gate_ref, down_ref, small_ref, small_scalar, table_h, in_h, mem_h, block_h, *refs
):
    attn_o, gate_o, down_o = refs[:8], refs[8:10], refs[10]
    gains_o, loss_o, in_o, mem_o, block_o, table_o = refs[11:15], refs[15], refs[16], refs[17], refs[18], refs[19]
    rounded, wide, in_v, mem_v, block_v, sems = refs[20:]
    copies = Copies(sems)
    rows = [pl.ds(i * CHUNK, min(CHUNK, vocab - i * CHUNK)) for i in range(rounded.shape[0] // CHUNK)]
    loads = [copies.start(table_h.at[where], rounded.at[where]) for where in rows]
    moved = [
        (copies.start(src, through), through, dst)
        for src, through, dst in ((in_h, in_v, in_o), (mem_h, mem_v, mem_o), (block_h, block_v, block_o))
    ]
    for where, load in zip(rows, loads):
        load.wait()
        wide[where, :] = rounded[where, :].astype(F32)
        copies.save(wide.at[where], table_o.at[where])
    for load, through, dst in moved:
        load.wait()
        copies.save(through, dst)
    for n, out in enumerate(attn_o):
        out[...] = attn_ref[n].astype(F32)
    for n, out in enumerate(gate_o):
        out[...] = gate_ref[n].astype(F32)
    narrow = down_ref.shape[2]
    for e in range(2):
        down_o[:, e * narrow : (e + 1) * narrow] = down_ref[e].astype(F32)
    depth = attn_ref.shape[1]
    width = small_ref.shape[1]
    turned = pltpu.roll(small_ref[...], width - lax.axis_index("wide") * depth, 1)
    for n, out in enumerate(gains_o):
        out[...] = turned[n : n + 1, 0:depth]
    loss_o[0, 0] = small_scalar[4, 0]
    copies.finish()


def finish(vocab, attn, gate, down, small, table, input_grad, memory_grad, block):
    depth, heads, units = attn.shape[1], attn.shape[2], gate.shape[2]
    vmem, hbm, smem = (pl.BlockSpec(memory_space=space) for space in (pltpu.VMEM, pl.ANY, pltpu.SMEM))
    high, width = table.shape

    def result(*shape):
        return jax.ShapeDtypeStruct(shape, F32)

    return pl.pallas_call(
        functools.partial(finish_kernel, vocab),
        out_shape=[result(depth, heads)] * 8 + [result(depth, units)] * 3 + [result(1, depth)] * 4 + [
            result(1, 1), result(*input_grad.shape), result(*memory_grad.shape),
            jax.ShapeDtypeStruct(block.shape, BF), result(vocab, width),
        ],
        in_specs=[vmem, vmem, vmem, vmem, smem] + [hbm] * 4,
        out_specs=[vmem] * 15 + [smem] + [hbm] * 4,
        scratch_shapes=[
            pltpu.VMEM((high, width), BF), pltpu.VMEM((high, width), F32), pltpu.VMEM(input_grad.shape, F32),
            pltpu.VMEM(memory_grad.shape, F32), pltpu.VMEM(block.shape, BF), pltpu.SemaphoreType.DMA((24,)),
        ],
        compiler_params=pltpu.CompilerParams(vmem_limit_bytes=VMEM_BYTES),
        name="finish",
    )(attn, gate, down, small, small, table, input_grad, memory_grad, block)


def fused_body(
    layer_input,
    memory,
    reader_map,
    target_ids,
    target_lengths,
    out_grad,
    self_q,
    self_k,
    self_v,
    self_o,
    cross_q,
    cross_k,
    cross_v,
    cross_o,
    ff_gate,
    ff_up,
    ff_out,
    gain_self,
    gain_cross,
    gain_ff,
    gain_exit,
    exit_table,
):
    count = lax.axis_size("wide")
    wide_index = lax.axis_index("wide")
    depth = gain_self.shape[0]
    group_map = reader_map[None, :]
    (
        block_output, resid_one, resid_two, resid_three, queries, keys, values, cross_queries, keys_read, values_read,
        context_self, context_cross, probs_self, probs_cross, gate_act, up_act, slots, attn_weights, gate_weights, down_weights,
        gains, exit_rows_grad, loss_part, table_half,
    ) = front(
        count, layer_input, memory, group_map, target_lengths, (gain_self, gain_cross, gain_ff, gain_exit), target_ids[None, :],
        (self_q, self_k, self_v, self_o, cross_q, cross_k, cross_v, cross_o, ff_gate, ff_up, ff_out), exit_table,
    )
    input_grad, memory_grad, small, attn_grads, gate_grads, down_grads, table_grad = backward_layer(
        count, target_lengths, group_map,
        (
            layer_input, out_grad, exit_rows_grad, loss_part, resid_one, resid_two, resid_three, queries, keys, values,
            cross_queries, keys_read, values_read, context_self, context_cross, probs_self, probs_cross, gate_act, up_act,
            slots, attn_weights, gate_weights, down_weights, gains,
        ),
        table_half,
    )
    done = finish(
        exit_table.shape[0], attn_grads, gate_grads, down_grads, small, table_grad, input_grad, memory_grad, block_output
    )
    attn, gate, down, gains, loss = done[:8], done[8:10], done[10], done[11:15], done[15]
    input_grad, memory_grad, block_output, table_grad = done[16:]
    return (
        block_output, loss[0, 0], input_grad, memory_grad, attn[0], attn[1], attn[2], attn[3], attn[6], attn[4], attn[5],
        attn[7], gate[0], gate[1], down, gains[0][0], gains[1][0], gains[2][0], gains[3][0], table_grad,
    )


def fits(mesh):
    return mesh.shape["wide"] == 4 and mesh.shape["tp"] == 2 and mesh.shape["grp"] == 4


def solution(mesh):
    placed = (
        P(("grp", "wide"), None),
        P(("grp", "wide"), None),
        P("grp"),
        P("grp"),
        P(),
        P(("grp", "wide"), None),
        P("wide", "tp"),
        P("wide", "tp"),
        P("wide", "tp"),
        P("wide", "tp"),
        P("wide", "tp"),
        P("wide", "tp"),
        P("wide", "tp"),
        P("wide", "tp"),
        P("wide", "tp"),
        P("wide", "tp"),
        P("wide", "tp"),
        P("wide"),
        P("wide"),
        P("wide"),
        P("wide"),
        P(("wide", "tp"), None),
    )
    return jax.shard_map(
        fused_body if fits(mesh) else plain_body,
        mesh=mesh,
        in_specs=placed,
        out_specs=(
            P(("grp", "wide"), None),
            P(),
            P(("grp", "wide"), None),
            P(("grp", "wide"), None),
            P("wide", "tp"),
            P("wide", "tp"),
            P("wide", "tp"),
            P("wide", "tp"),
            P("wide", "tp"),
            P("wide", "tp"),
            P("wide", "tp"),
            P("wide", "tp"),
            P("wide", "tp"),
            P("wide", "tp"),
            P("wide", "tp"),
            P("wide"),
            P("wide"),
            P("wide"),
            P("wide"),
            P(("wide", "tp"), None),
        ),
        check_vma=False,
    )
```

profile of v0, /device:TPU:21, one launch (start us, length us, event | category | flops | bytes accessed | tf_op | source)
XLA Modules:
  0.0 274.1 jit_solution(5937614200317603447)
XLA Ops:
  0.7 141.7 %forward_and_exit.1 = (bf16[256,768]{1,0:T(8,128)(2,1)}, f32[256,768]{1,0:T(8,128)}, f32[256,768]{1,0:T(8,128)}, f32[256,768]{1,0:T(8,128)}, bf16[256,384]{1,0:T...) custom-call(bf16[256,768]{1,0:T(8,128)(2,1)} %x_h.1, ...), custom_call_target="tpu_custom_call" | custom-call | tf_op jit(solution)/shard_map/forward_and_exit/pallas_call | solution.py:1103
  142.4 120.4 %backward_layer.1 = (f32[256,768]{1,0:T(8,128)}, f32[256,768]{1,0:T(8,128)}, f32[8,768]{1,0:T(8,128)}, bf16[8,192,384]{2,1,0:T(8,128)(2,1)}, bf16[2,192,1024]{2,...) custom-call(s32[16]{0:T(128)} %lens.1, s32[1,1024]{1,0:T(1,128)} %bitcast.8, ...), custom_call_target="tpu_custom_call" | custom-call | tf_op jit(solution)/shard_map/backward_layer/pallas_call | solution.py:1484
  262.8 11.1 %finish.1 = (f32[192,384]{1,0:T(8,128)}, f32[192,384]{1,0:T(8,128)}, f32[192,384]{1,0:T(8,128)}, f32[192,384]{1,0:T(8,128)}, f32[192,384]{1,0:T(8,128)}, /*index...) custom-call(bf16[8,192,384]{2,1,0:T(8,128)(2,1)} %get-tuple-element., ...), custom_call_target="tpu_custom_call" | custom-call | tf_op jit(solution)/shard_map/finish/pallas_call | solution.py:1546
where the time goes:
time: 279 us; the launch traced here: 274 us
  Pallas kernels  273 us (98%)
    pallas_call x1, Pallas kernels, front(): pl.pallas_call(functools.partial(front_kernel, count, vocab), out_shape=[...  142 us
    pallas_call x1, Pallas kernels, backward_layer(): pl.pallas_call(functools.partial(backward_kernel, count), out_shape=[jax....  120 us
    pallas_call x1, Pallas kernels, finish(): pl.pallas_call(functools.partial(finish_kernel, vocab), out_shape=[result...  11.1 us

commit v1 on v0

--- a/solution.py
+++ b/solution.py
@@ -484,6 +484,7 @@
 
     def move(self, src, dst, device, lands):
         k = self.used
+        assert k < self.send_sems.shape[0]
         self.used += 1
         out = pltpu.make_async_remote_copy(
             src_ref=src, dst_ref=dst, send_sem=self.send_sems.at[k], recv_sem=self.recv_sems.at[k],
@@ -512,6 +513,7 @@
         self.sems, self.used, self.pending = sems, 0, []
 
     def start(self, src, dst):
+        assert self.used < self.sems.shape[0]
         made = pltpu.make_async_copy(src, dst, self.sems.at[self.used])
         self.used += 1
         made.start()
@@ -663,6 +665,7 @@
 
 
 CHUNK = 512
+CROSSED = 1
 
 
 def tall(rows):
@@ -681,7 +684,7 @@
     lax.fori_loop(0, tab.shape[0] // CHUNK, step, 0)
 
 
-def exit_phase(here, links, rows_own, tab, tabt, gt, rb, ids, lens, high, total, stats, stats_tp, stats_wide, coef, weight, acc,
+def exit_phase(here, links, rows_own, tab, tabt, gt, rb, ids, lens, high, total, stats, packed_stats, stats_tp, stats_wide, coef, weight, acc,
                dx, joint, land_tp, land_far, land_near, swap_out, swap_in, grad_out, vocab, fillers):
     count, g, w, t = here.count, here.g, here.w, here.t
     left, right, far = here.left, here.right, here.far
@@ -757,15 +760,20 @@
     far_rest.landed()
     score(far)
 
+    lines = tokens // 128
+
     def merged_stats(parts):
-        top = parts[0][0:1]
+        top = parts[0][0:lines]
         for part in parts[1:]:
-            top = jnp.maximum(top, part[0:1])
-        mass = sum(part[1:2] * jnp.exp(part[0:1] - top) for part in parts)
-        pick = sum(part[2:3] for part in parts)
+            top = jnp.maximum(top, part[0:lines])
+        mass = sum(part[lines : 2 * lines] * jnp.exp(part[0:lines] - top) for part in parts)
+        pick = sum(part[2 * lines :] for part in parts)
         return top, mass, pick
 
-    swap = links.move(stats, stats_tp, to_tp, stats_tp).start()
+    for n in range(3):
+        for line in range(lines):
+            packed_stats[n * lines + line : n * lines + line + 1, :] = stats[n : n + 1, line * 128 : (line + 1) * 128]
+    swap = links.move(packed_stats, stats_tp, to_tp, stats_tp).start()
     lengths = [lens[k] for k in range(lens.shape[0])]
     tokens_all = lengths[0]
     for length in lengths[1:]:
@@ -775,12 +783,11 @@
         inside = jnp.where(place < lens[g * count + b], 1.0, 0.0).astype(F32)
         weight[0:1, b * rows : (b + 1) * rows] = inside / tokens_all.astype(F32)
     swap.landed()
-    mine, other = stats[...], stats_tp[...]
-    top, mass, pick = merged_stats([mine, other])
+    top, mass, pick = merged_stats([packed_stats[...], stats_tp[...]])
     mine_wide = stats_wide.at[w]
-    mine_wide[0:1, :] = top
-    mine_wide[1:2, :] = mass
-    mine_wide[2:3, :] = pick
+    mine_wide[0:lines, :] = top
+    mine_wide[lines : 2 * lines, :] = mass
+    mine_wide[2 * lines :, :] = pick
     spreads = [
         links.move(mine_wide, mine_wide, device, stats_wide.at[at]).start()
         for device, at in ((to_left, right), (to_right, left), (to_far, far))
@@ -789,10 +796,15 @@
         made.landed()
     top, mass, pick = merged_stats([stats_wide[b] for b in range(count)])
     log_total = top + jnp.log(mass)
+    token_loss = log_total - pick
+    for line in range(lines):
+        cols = slice(line * 128, (line + 1) * 128)
+        stats[3:4, cols] = log_total[line : line + 1]
+        stats[4:5, cols] = token_loss[line : line + 1]
     all_weight = weight[0:1, :]
-    coef[...] = jnp.exp(high[...] - log_total) * all_weight
-    stats_tp[3:4, :] = (log_total - pick) * all_weight
-    loss = jnp.sum(stats_tp[3:4, block(w)], axis=1, keepdims=True)
+    coef[...] = jnp.exp(high[...] - stats[3:4, :]) * all_weight
+    stats[5:6, :] = stats[4:5, :] * all_weight
+    loss = jnp.sum(stats[5:6, block(w)], axis=1, keepdims=True)
 
     def row_grads(b):
         cols = block(b)
@@ -860,12 +872,12 @@
 
 
 class TableGrad:
-    def __init__(self, here, links, copies, tab, gt, rb, land_core, out):
+    def __init__(self, here, links, copies, tab, gt, rb, land_core, land_y, out):
         self.here, self.links, self.copies = here, links, copies
-        self.tab, self.gt, self.rb, self.land_core, self.out = tab, gt, rb, land_core, out
+        self.tab, self.gt, self.rb, self.land_core, self.land_y, self.out = tab, gt, rb, land_core, land_y, out
         self.pieces = tab.shape[0] // (2 * CHUNK)
         self.scale = float(tab.shape[1]) ** (-0.5)
-        self.cores = []
+        self.cores, self.ys = [], []
 
     def rows(self, owner, i):
         return pl.ds(pl.multiple_of((owner * self.pieces + i) * CHUNK, CHUNK), CHUNK)
@@ -873,22 +885,41 @@
     def product(self, where):
         return dot_nn(self.gt[where, :], self.rb[...]) * self.scale
 
-    def first_half(self):
-        c = self.here.c
+    def give(self, i):
+        where = self.rows(1 - self.here.c, i)
+        self.tab[where, :] = self.product(where).astype(BF)
+        land = self.land_core.at[pl.ds(i * CHUNK, CHUNK)]
+        self.cores.append(self.links.move(self.tab.at[where], land, self.here.to_core, land).start())
+
+    def take(self, i):
+        where = self.rows(self.here.c, i)
+        mine = self.product(where)
+        self.cores[i].landed()
+        self.tab[where, :] = (mine + self.land_core[i * CHUNK : (i + 1) * CHUNK, :].astype(F32)).astype(BF)
+        if i < CROSSED:
+            land = self.land_y.at[pl.ds(i * CHUNK, CHUNK)]
+            self.ys.append(self.links.move(self.tab.at[where], land, self.here.to_y, land).start())
+        else:
+            self.copies.save(self.tab.at[where], self.out.at[pl.ds(i * CHUNK, CHUNK)])
+
+    def first(self):
         for i in range(self.pieces):
-            where = self.rows(1 - c, i)
-            self.tab[where, :] = self.product(where).astype(BF)
-            land = self.land_core.at[pl.ds(i * CHUNK, CHUNK)]
-            self.cores.append(self.links.move(self.tab.at[where], land, self.here.to_core, land).start())
-
-    def second_half(self):
-        c = self.here.c
-        for i in range(self.pieces):
-            where = self.rows(c, i)
-            mine = self.product(where)
-            self.cores[i].landed()
-            self.tab[where, :] = (mine + self.land_core[i * CHUNK : (i + 1) * CHUNK, :].astype(F32)).astype(BF)
-            self.copies.save(self.tab.at[where], self.out.at[pl.ds(i * CHUNK, CHUNK)])
+            self.give(i)
+        for i in range(CROSSED):
+            self.take(i)
+
+    def second(self):
+        for i in range(CROSSED, self.pieces):
+            self.take(i)
+
+    def settle(self):
+        for i in range(CROSSED):
+            where = self.rows(self.here.c, i)
+            piece = pl.ds(i * CHUNK, CHUNK)
+            self.ys[i].landed()
+            self.ys[i].sent()
+            self.tab[where, :] = (self.tab[where, :].astype(F32) + self.land_y[piece, :].astype(F32)).astype(BF)
+            self.copies.save(self.tab.at[where], self.out.at[piece])
 
 
 def front_kernel(
@@ -898,8 +929,8 @@
     ga_o, up_o, sel_o, wa_o, wgu_o, wd_o, gain_o, grad_o, loss_o, half_o,
     wa, wgu, wd, gains, slots, packed, part_out, part_in, valid_slot,
     block, one, two, three, q, k, v, cq, mk, mv, sc, cc, ps, pc, ga, up, gain_sum, exit_rows,
-    tab, tabt, gt, rb, high_v, total, stats, stats_tp, stats_wide, coef, weight, acc, dx, joint, land_tp, land_far, land_near,
-    swap_out, swap_in, land_core,
+    tab, tabt, gt, rb, high_v, total, stats, packed_stats, stats_tp, stats_wide, coef, weight, acc, dx, joint, land_tp, land_far, land_near,
+    swap_out, swap_in, land_core, land_y,
     send_sems, recv_sems, copy_sems,
 ):
     here = position(count)
@@ -935,7 +966,7 @@
         links.move(gains.at[w], gains.at[w], device, gains.at[at]).start()
         for device, at in ((to_left, right), (to_right, left), (to_far, far))
     ]
-    for first in weights[:3]:
+    for first in weights[:2]:
         first.issue()
 
     capacity = slots.shape[0] // count
@@ -948,7 +979,7 @@
     own_slots = pl.ds(pl.multiple_of(w * capacity, 16), capacity)
     slots[own_slots, :] = packed[own_slots, :]
     weights[0].forward()
-    weights[3].issue()
+    weights[2].issue()
     for made in gain_moves:
         made.landed()
     total_gain = gains[0]
@@ -959,14 +990,15 @@
     norm_self = rms_rows(hidden, gain_sum[0:1, :])
     weights[1].forward()
     weights[0].complete()
+    weights[3].issue()
+    weights[2].forward()
+    weights[0].share()
+    weights[1].complete()
+    weights[1].share()
     slot_moves = [
         links.move(packed.at[slot_rows(to, t)], slots.at[slot_rows(w, t)], device, slots.at[slot_rows(at, t)]).start()
         for device, to, at in ((to_left, left, right), (to_right, right, left), (to_far, far, far))
     ]
-    weights[2].forward()
-    weights[0].share()
-    weights[1].complete()
-    weights[1].share()
     weights[4].issue()
     weights[0].ready()
     q[...] = dot_nn(norm_self, wa[0]).astype(BF)
@@ -1059,13 +1091,14 @@
     exit_rows[...] = rms_rows(three[...], gain_sum[3:4, :])
     copies.save(three, three_o)
     copies.save(block, block_o)
-    grads = TableGrad(here, links, copies, tab, gt, rb, land_core, half_o)
+    grads = TableGrad(here, links, copies, tab, gt, rb, land_core, land_y, half_o)
     loss = exit_phase(
-        here, links, exit_rows, tab, tabt, gt, rb, ids, len_ref, high_v, total, stats, stats_tp, stats_wide, coef, weight, acc,
-        dx, joint, land_tp, land_far, land_near, swap_out, swap_in, grad_o, vocab, (grads.first_half, grads.second_half),
+        here, links, exit_rows, tab, tabt, gt, rb, ids, len_ref, high_v, total, stats, packed_stats, stats_tp, stats_wide, coef, weight, acc,
+        dx, joint, land_tp, land_far, land_near, swap_out, swap_in, grad_o, vocab, (grads.first, grads.second),
     )
     loss_o[...] = jnp.broadcast_to(loss, loss_o.shape)
-    links.finish()
+    grads.settle()
+    links.finish_rest(grads.ys)
     copies.finish()
 
 
@@ -1094,10 +1127,11 @@
     scratch += [
         ((8, width), F32), ((rows, width), BF),
         ((high, width), BF), ((width, high), BF), ((high, tokens), BF), ((tokens, width), BF), ((chunks, tokens), F32),
-        ((chunks, tokens), F32), ((8, tokens), F32), ((8, tokens), F32), ((count, 8, tokens), F32), ((chunks, tokens), F32),
+        ((chunks, tokens), F32), ((8, tokens), F32), ((3 * tokens // 128, 128), F32), ((3 * tokens // 128, 128), F32),
+        ((count, 3 * tokens // 128, 128), F32), ((chunks, tokens), F32),
         ((8, tokens), F32), ((width, rows), F32), ((4, rows, width), BF), ((4, rows // 2, width), BF), ((4, rows // 2, width), BF),
         ((2, rows // 4, width), BF), ((2, rows // 2, width), BF), ((rows // 2, width), BF), ((rows // 2, width), BF),
-        ((high // 2, width), BF),
+        ((high // 2, width), BF), ((max(16, CROSSED * CHUNK), width), BF),
     ]
     results = kept + [((rows, width), F32), ((8, 128), F32), ((high // 2, width), BF)]
     return pl.pallas_call(
@@ -1224,6 +1258,83 @@
         self.share.landed()
 
 
+class LateWeightGrad(WeightGrad):
+    def quarter(self, at, which):
+        size = self.depth // 4
+        return pl.ds(pl.multiple_of(at * self.depth + (2 * self.here.yy + which) * size, 16), size)
+
+    def cross(self, land_early):
+        here = self.here
+        self.core.landed()
+        self.crossings = []
+        self.land_early = land_early
+        for at in range(here.count):
+            self.add_core(self.whole(at))
+            src, land = self.grads.at[self.mine, self.part(at, 1 - here.yy)], land_early.at[at]
+            self.crossings.append(self.links.move(src, land, here.to_y, land).start())
+
+    def near(self, where, side, which, device):
+        rows = pl.ds(which * (self.half // 2), self.half // 2)
+        return self.links.move(
+            self.grads.at[self.mine, where], self.land_near.at[side, rows], device, self.land_near.at[side, rows]
+        ).start()
+
+    def far_land(self, which):
+        return self.land_far.at[which, pl.ds(0, self.half // 2)]
+
+    def ring(self):
+        here = self.here
+        for at, made in enumerate(self.crossings):
+            made.landed()
+            where = self.part(at, here.yy)
+            self.grads[self.mine, where] = (
+                self.grads[self.mine, where].astype(F32) + self.land_early[at].astype(F32)
+            ).astype(BF)
+        self.far = [
+            self.links.move(
+                self.grads.at[self.mine, self.quarter(here.far, e)], self.far_land(e), way, self.far_land(e)
+            ).start()
+            for e, way in enumerate((here.to_right, here.to_left))
+        ]
+        self.early = [
+            self.near(self.quarter(here.right, 1), 0, 1, here.to_right),
+            self.near(self.quarter(here.left, 0), 1, 0, here.to_left),
+        ]
+
+    def pass_on(self):
+        here = self.here
+        self.late = []
+        for e, side, way in ((0, here.right, here.to_right), (1, here.left, here.to_left)):
+            self.far[e].landed()
+            where = self.quarter(side, e)
+            self.grads[self.mine, where] = (
+                self.grads[self.mine, where].astype(F32) + self.far_land(e)[...].astype(F32)
+            ).astype(BF)
+            self.late.append(self.near(where, e, e, way))
+
+    def across(self):
+        here = self.here
+        for made in self.early + self.late:
+            made.landed()
+        where = self.part(here.w, here.yy)
+        own, other = (pl.ds(pl.multiple_of(y * self.half, 16), self.half) for y in (here.yy, 1 - here.yy))
+        self.mine_out[1, own] = (
+            self.grads[self.mine, where].astype(F32)
+            + self.land_near[0, 0 : self.half].astype(F32)
+            + self.land_near[1, 0 : self.half].astype(F32)
+        ).astype(BF)
+        src = self.mine_out.at[1, own]
+        self.y = self.links.move(src, src, here.to_y, self.mine_out.at[1, other]).start()
+
+    def settle(self):
+        self.y.landed()
+        src = self.mine_out.at[1]
+        self.copies.save(src, self.out.at[self.mine])
+        self.share = self.links.move(
+            src, self.out.at[self.mine], self.here.to_core, self.out.at[self.other]
+        ).start()
+
+
 def backward_kernel(
     count,
     lens, map_ref, x_h, og_h, eg_h, loss_h, one_h, two_h, three_h, q_h, k_h, v_h, cq_h, mk_h, mv_h, sc_h, cc_h, ps_h, pc_h,
@@ -1231,7 +1342,7 @@
     in_o, mem_o, small_o, ga8_o, ggu_o, gd_o, table_o,
     x, og, eg, loss, one, two, three, q, k, v, cq, mk, mv, sc, cc, ps, pc, ga, up, sel, wa, wgu, wd, gain, tab, land_t,
     part_out, part_in, grad, dq, dk, dv, dmk, dmv, dctx, gate_grad, up_grad, ff_hidden,
-    g8, ggu, gd, lc8, lcg, lcd, lf8, lfg, lfd, ln8, lng, lnd, ly8, lyg, lyd, mo8, mog, mod,
+    g8, ggu, gd, lc8, lcg, lcd, lf8, lfg, lfd, ln8, lng, lnd, ly8, lyg, lyd, mo8, mog, mod, land_early,
     back_slots, land_slots, got_slots, small, small_wide, small_land,
     send_sems, recv_sems, copy_sems,
 ):
@@ -1257,15 +1368,16 @@
     need(tab)
     crossing = [
         links.move(tab.at[pl.ds(i * CHUNK, CHUNK)], land_t.at[pl.ds(i * CHUNK, CHUNK)], here.to_y, land_t.at[pl.ds(i * CHUNK, CHUNK)]).start()
-        for i in range(pieces)
+        for i in range(CROSSED, pieces)
     ]
     shares = []
 
     def settle_table(i):
         piece = pl.ds(i * CHUNK, CHUNK)
-        crossing[i].landed()
-        crossing[i].sent()
-        tab[piece, :] = (tab[piece, :].astype(F32) + land_t[piece, :].astype(F32)).astype(BF)
+        if i >= CROSSED:
+            crossing[i - CROSSED].landed()
+            crossing[i - CROSSED].sent()
+            tab[piece, :] = (tab[piece, :].astype(F32) + land_t[piece, :].astype(F32)).astype(BF)
 
         def rows(owner):
             return pl.ds(pl.multiple_of((owner * pieces + i) * CHUNK, CHUNK), CHUNK)
@@ -1279,7 +1391,8 @@
 
     def weight_pair(i):
         if i < 4:
-            return WeightGrad(here, links, copies, g8, 2 * i, depth, lc8.at[i], lf8.at[i], ln8.at[i], ly8.at[i], mo8.at[i], ga8_o)
+            kind = LateWeightGrad if i < 2 else WeightGrad
+            return kind(here, links, copies, g8, 2 * i, depth, lc8.at[i], lf8.at[i], ln8.at[i], ly8.at[i], mo8.at[i], ga8_o)
         if i == 4:
             return WeightGrad(here, links, copies, ggu, 0, depth, lcg, lfg, lng, lyg, mog, ggu_o)
         return WeightGrad(here, links, copies, gd, 0, depth, lcd, lfd, lnd, lyd, mod, gd_o)
@@ -1327,6 +1440,8 @@
     for e in range(2):
         gd[e] = dot_nn(branch_rows, ff_hidden[:, e * units : (e + 1) * units]).astype(BF)
     pair[5].pair()
+    for i in range(CROSSED):
+        settle_table(i)
     pair[4].ring()
     gain_row, back = norm_back(two[...], gain[2:3, :], exchanged(0, swap))
     small[2:3, :] = gain_row
@@ -1382,6 +1497,7 @@
     attention_backward(pairs, q, k, v, ps, dctx, dq, dk, dv)
     part_out[2] = (dot_nt(dq[...], wa[0]) + dot_nt(dk[...], wa[1]) + dot_nt(dv[...], wa[2])).astype(BF)
     swap = exchange_start(2)
+    pair[4].across()
     hidden = x[...].astype(F32)
     norm_t = rms_rows(hidden, gain[0:1, :]).T
     g8[0] = dot_nn(norm_t, dq[...]).astype(BF)
@@ -1392,9 +1508,8 @@
     pair[1].pair()
     pair[3].pass_on()
     pair[2].pass_on()
-    pair[0].ring()
-    pair[1].ring()
-    pair[4].across()
+    pair[0].cross(land_early.at[0])
+    pair[1].cross(land_early.at[1])
     pair[5].across()
     for made in returns:
         made.landed()
@@ -1406,6 +1521,8 @@
     small[0:1, :] = gain_row
     grad[...] += back
     copies.save(grad, in_o)
+    pair[0].ring()
+    pair[1].ring()
     need(loss)
     small[4:5, 0:128] = loss[0:1, :]
 
@@ -1414,6 +1531,7 @@
         links.move(small, small_wide.at[w], device, small_wide.at[at]).start()
         for device, at in ((to_left, here.right), (to_right, here.left), (to_far, here.far))
     ]
+    settle_table(CROSSED)
     pair[0].pass_on()
     pair[1].pass_on()
     pair[3].across()
@@ -1433,7 +1551,7 @@
         total = total + small_land[2 * n + 1]
     small_o[...] = total
     mem_o[...] = exchanged(3, memory_swap)
-    for i in range(pieces):
+    for i in range(CROSSED + 1, pieces):
         settle_table(i)
     for i in (4, 5, 3, 2, 0, 1):
         pair[i].settle()
@@ -1476,10 +1594,11 @@
     scratch += three_kinds(depth, (2,))
     scratch += three_kinds(depth)
     scratch += three_kinds(depth, (2,))
+    scratch += [pltpu.VMEM((2, count, half, heads), BF)]
     scratch += [
         pltpu.VMEM((2, slots // 2, width), BF), pltpu.VMEM((slots // 2, width), BF), pltpu.VMEM((slots // 2, width), BF), pltpu.VMEM((8, width), F32),
         pltpu.VMEM((count, 8, width), F32), pltpu.VMEM((4, 8, width), F32),
-        pltpu.SemaphoreType.DMA((80,)), pltpu.SemaphoreType.DMA((80,)), pltpu.SemaphoreType.DMA((48,)),
+        pltpu.SemaphoreType.DMA((96,)), pltpu.SemaphoreType.DMA((96,)), pltpu.SemaphoreType.DMA((48,)),
     ]
     return pl.pallas_call(
         functools.partial(backward_kernel, count),
@@ -1500,18 +1619,31 @@
 
 
 def finish_kernel(
-    vocab, attn_ref, gate_ref, down_ref, small_ref, small_scalar, table_h, in_h, mem_h, block_h, *refs
+    vocab, small_ref, small_scalar, attn_h, gate_h, down_h, table_h, in_h, mem_h, block_h, *refs
 ):
     attn_o, gate_o, down_o = refs[:8], refs[8:10], refs[10]
     gains_o, loss_o, in_o, mem_o, block_o, table_o = refs[11:15], refs[15], refs[16], refs[17], refs[18], refs[19]
-    rounded, wide, in_v, mem_v, block_v, sems = refs[20:]
+    rounded, wide, in_v, mem_v, block_v, attn_ref, gate_ref, down_ref, attn_v, gate_v, down_v, sems = refs[20:]
     copies = Copies(sems)
     rows = [pl.ds(i * CHUNK, min(CHUNK, vocab - i * CHUNK)) for i in range(rounded.shape[0] // CHUNK)]
+    small_loads = [copies.start(src, dst) for src, dst in ((attn_h, attn_ref), (gate_h, gate_ref), (down_h, down_ref))]
     loads = [copies.start(table_h.at[where], rounded.at[where]) for where in rows]
     moved = [
         (copies.start(src, through), through, dst)
         for src, through, dst in ((in_h, in_v, in_o), (mem_h, mem_v, mem_o), (block_h, block_v, block_o))
     ]
+    for load in small_loads:
+        load.wait()
+    narrow = down_ref.shape[2]
+    for n, out in enumerate(attn_o):
+        attn_v[n] = attn_ref[n].astype(F32)
+        copies.save(attn_v.at[n], out)
+    for n, out in enumerate(gate_o):
+        gate_v[n] = gate_ref[n].astype(F32)
+        copies.save(gate_v.at[n], out)
+    for e in range(2):
+        down_v[:, e * narrow : (e + 1) * narrow] = down_ref[e].astype(F32)
+    copies.save(down_v, down_o)
     for where, load in zip(rows, loads):
         load.wait()
         wide[where, :] = rounded[where, :].astype(F32)
@@ -1519,13 +1651,6 @@
     for load, through, dst in moved:
         load.wait()
         copies.save(through, dst)
-    for n, out in enumerate(attn_o):
-        out[...] = attn_ref[n].astype(F32)
-    for n, out in enumerate(gate_o):
-        out[...] = gate_ref[n].astype(F32)
-    narrow = down_ref.shape[2]
-    for e in range(2):
-        down_o[:, e * narrow : (e + 1) * narrow] = down_ref[e].astype(F32)
     depth = attn_ref.shape[1]
     width = small_ref.shape[1]
     turned = pltpu.roll(small_ref[...], width - lax.axis_index("wide") * depth, 1)
@@ -1549,15 +1674,18 @@
             result(1, 1), result(*input_grad.shape), result(*memory_grad.shape),
             jax.ShapeDtypeStruct(block.shape, BF), result(vocab, width),
         ],
-        in_specs=[vmem, vmem, vmem, vmem, smem] + [hbm] * 4,
-        out_specs=[vmem] * 15 + [smem] + [hbm] * 4,
+        in_specs=[vmem, smem] + [hbm] * 7,
+        out_specs=[hbm] * 11 + [vmem] * 4 + [smem] + [hbm] * 4,
         scratch_shapes=[
             pltpu.VMEM((high, width), BF), pltpu.VMEM((high, width), F32), pltpu.VMEM(input_grad.shape, F32),
-            pltpu.VMEM(memory_grad.shape, F32), pltpu.VMEM(block.shape, BF), pltpu.SemaphoreType.DMA((24,)),
+            pltpu.VMEM(memory_grad.shape, F32), pltpu.VMEM(block.shape, BF),
+            pltpu.VMEM(attn.shape, BF), pltpu.VMEM(gate.shape, BF), pltpu.VMEM(down.shape, BF),
+            pltpu.VMEM(attn.shape, F32), pltpu.VMEM(gate.shape, F32), pltpu.VMEM((depth, units), F32),
+            pltpu.SemaphoreType.DMA((40,)),
         ],
         compiler_params=pltpu.CompilerParams(vmem_limit_bytes=VMEM_BYTES),
         name="finish",
-    )(attn, gate, down, small, small, table, input_grad, memory_grad, block)
+    )(small, small, attn, gate, down, table, input_grad, memory_grad, block)
 
 
 def fused_body(

time: 279 us -> 274 us (0.982)
  the two profiles are of different devices: /device:TPU:21 before, /device:TPU:19 now
where the time goes in v1:
time: 274 us; the launch traced here: 269 us
  Pallas kernels  269 us (98%)
    pallas_call x1, Pallas kernels, front(): pl.pallas_call(functools.partial(front_kernel, count, vocab), out_shape=[...  149 us
    pallas_call x1, Pallas kernels, backward_layer(): pl.pallas_call(functools.partial(backward_kernel, count), out_shape=[jax....  108 us
    pallas_call x1, Pallas kernels, finish(): pl.pallas_call(functools.partial(finish_kernel, vocab), out_shape=[result...  11.4 us

profile of v1, /device:TPU:19, one launch (start us, length us, event | category | flops | bytes accessed | tf_op | source)
XLA Modules:
  0.0 269.5 jit_solution(13013325806216918714)
XLA Ops:
  0.7 149.2 %forward_and_exit.1 = (bf16[256,768]{1,0:T(8,128)(2,1)}, f32[256,768]{1,0:T(8,128)}, f32[256,768]{1,0:T(8,128)}, f32[256,768]{1,0:T(8,128)}, bf16[256,384]{1,0:T...) custom-call(bf16[256,768]{1,0:T(8,128)(2,1)} %x_h.1, ...), custom_call_target="tpu_custom_call" | custom-call | tf_op jit(solution)/shard_map/forward_and_exit/pallas_call | solution.py:1137
  149.9 108.0 %backward_layer.1 = (f32[256,768]{1,0:T(8,128)}, f32[256,768]{1,0:T(8,128)}, f32[8,768]{1,0:T(8,128)}, bf16[8,192,384]{2,1,0:T(8,128)(2,1)}, bf16[2,192,1024]{2,...) custom-call(s32[16]{0:T(128)} %lens.1, s32[1,1024]{1,0:T(1,128)} %bitcast.8, ...), custom_call_target="tpu_custom_call" | custom-call | tf_op jit(solution)/shard_map/backward_layer/pallas_call | solution.py:1603
  257.8 11.4 %finish.1 = (f32[192,384]{1,0:T(8,128)}, f32[192,384]{1,0:T(8,128)}, f32[192,384]{1,0:T(8,128)}, f32[192,384]{1,0:T(8,128)}, f32[192,384]{1,0:T(8,128)}, /*index...) custom-call(f32[8,768]{1,0:T(8,128)} %get-tuple-element.94.small_ref, ...), custom_call_target="tpu_custom_call" | custom-call | tf_op jit(solution)/shard_map/finish/pallas_call | solution.py:1671
